TPU v7x, 32 devices: a whole 2x2x4 slice. The times are simulated.
32 devices in a mesh: groups: 2 (over y), expert: 16 (over z, x, core), dp: 1.
Axes of the slice: x: 2, y: 2, z: 4, core: 2. Of those that a mesh axis runs over, the one named last changes fastest.
Arguments:
- grad_out: bfloat16 [4096, 2048], P(('groups', 'expert', 'dp')), parts along dimension 0, may hold values from -6 to 6
- hidden: bfloat16 [4096, 8, 384], P(('groups', 'expert', 'dp')), parts along dimension 0, may hold values from -0.29882812 to 0.29882812
- routes: int32 [4096, 8], P(('groups', 'expert', 'dp')), parts along dimension 0, may hold values from 0 to 15, all different within a row; in each aligned block of 128 rows (0 to 127, 128 to 255, ...) at most 128 rows name the same one
- probs: bfloat16 [4096, 8], P(('groups', 'expert', 'dp')), parts along dimension 0, may hold values from 0.019897461 to 0.29882812
- w_down: bfloat16 [16, 384, 2048], P('expert', 'dp'), may hold values from -0.3125 to 0.3125
Outputs:
- grad_hidden: bfloat16 [4096, 8, 384], P(('groups', 'expert', 'dp')), parts along dimension 0
- grad_probs: bfloat16 [4096, 8], P(('groups', 'expert', 'dp')), parts along dimension 0
- grad_w: bfloat16 [32, 384, 2048], P(('groups', 'expert'), 'dp'), parts along dimension 0
There are 2 independent parts, one for each index of `groups`. A program takes and returns all parts, laid end to end along the dimension named above; an argument that names none is the same for every part. Nothing has to cross between parts.
Inputs may be any that keep to these rules, and one draw needn't show every extreme that they name: `routes`: each token names 8 different experts. In each aligned block of 128 rows (the tokens of one device) no expert is named by more than 128 rows, a bound that some block reaches.
All inputs are finite; a program needn't handle non-finite values.
Results may differ from a plain program's by a relative error of at most 0.012.
Values may be sent and summed in bfloat16 or wider, within the bound.
No kernel may reach another device: no remote copies, remote signals or barrier semaphores. Data moves between devices by JAX's collectives and lax.ppermute only.
A program may use at most 64 MiB of HBM per device.

v0:
```python
import jax
import jax.numpy as jnp
from jax import lax
from jax.sharding import PartitionSpec as P


def on_device(grad_out, hidden, routes, probs, w_down):
    token_count, model_width = grad_out.shape
    top_count = routes.shape[1]
    inner_width = hidden.shape[2]
    peer_count = lax.axis_size("expert")
    capacity = min(token_count, max(2, 2 * token_count * top_count // peer_count))
    slot_count = token_count * top_count
    row_count = peer_count * capacity
    flat_ids = routes.reshape(slot_count)
    expert_row = jnp.arange(peer_count, dtype=jnp.int32)
    onehot = (flat_ids[:, None] == expert_row[None, :]).astype(jnp.int32)
    before = jnp.cumsum(onehot, axis=0) - onehot
    slot_rank = jnp.sum(before * onehot, axis=1)
    target = flat_ids * capacity + slot_rank
    slot_table = (
        jnp.full((row_count,), slot_count, jnp.int32)
        .at[target]
        .set(jnp.arange(slot_count, dtype=jnp.int32))
    )
    token_index = jnp.where(slot_table < slot_count, slot_table // top_count, token_count)
    grad_ext = jnp.concatenate([grad_out, jnp.zeros((1, model_width), grad_out.dtype)])
    hidden_ext = jnp.concatenate(
        [hidden.reshape(slot_count, inner_width), jnp.zeros((1, inner_width), hidden.dtype)]
    )
    probs_ext = jnp.concatenate([probs.reshape(slot_count), jnp.zeros((1,), probs.dtype)])
    send_grad = grad_ext[token_index].reshape(peer_count, capacity, model_width)
    send_hidden = hidden_ext[slot_table].reshape(peer_count, capacity, inner_width)
    send_probs = probs_ext[slot_table].reshape(peer_count, capacity)
    local_weight = w_down[0]
    half_width = local_weight.shape[0]
    got_grad, got_hidden, got_probs = (
        lax.all_to_all(send_grad, "expert", split_axis=0, concat_axis=0, tiled=True),
        lax.all_to_all(send_hidden, "expert", split_axis=0, concat_axis=0, tiled=True),
        lax.all_to_all(send_probs, "expert", split_axis=0, concat_axis=0, tiled=True),
    )
    grad_rows = got_grad.reshape(row_count, model_width)
    hidden_rows = got_hidden.reshape(row_count, inner_width)
    prob_rows = got_probs.reshape(row_count)
    back_rows = lax.dot_general(
        grad_rows,
        lax.all_gather(local_weight, "dp", axis=0, tiled=True),
        (((1,), (1,)), ((), ())),
        preferred_element_type=jnp.float32,
    )
    prob_grads = jnp.sum(back_rows * hidden_rows.astype(jnp.float32), axis=1).astype(jnp.bfloat16)
    hidden_grads = (prob_rows.astype(jnp.float32)[:, None] * back_rows).astype(jnp.bfloat16)
    weighted = grad_rows * prob_rows[:, None]
    returned_hidden, returned_probs = (
        lax.all_to_all(
            hidden_grads.reshape(peer_count, capacity, inner_width),
            "expert",
            split_axis=0,
            concat_axis=0,
            tiled=True,
        ),
        lax.all_to_all(
            prob_grads.reshape(peer_count, capacity),
            "expert",
            split_axis=0,
            concat_axis=0,
            tiled=True,
        ),
    )
    summed = lax.psum_scatter(
        lax.dot_general(
            hidden_rows, weighted, (((0,), (0,)), ((), ())), preferred_element_type=jnp.float32
        ).astype(jnp.bfloat16),
        "dp",
        scatter_dimension=0,
        tiled=True,
    )
    grad_w = summed.reshape(1, half_width, model_width)
    grad_hidden = returned_hidden.reshape(row_count, inner_width)[target].reshape(
        token_count, top_count, inner_width
    )
    grad_probs = returned_probs.reshape(row_count)[target].reshape(token_count, top_count)
    return (grad_hidden, grad_probs, grad_w)


def solution(mesh):
    in_specs = (
        P(("groups", "expert", "dp"), None),
        P(("groups", "expert", "dp"), None, None),
        P(("groups", "expert", "dp"), None),
        P(("groups", "expert", "dp"), None),
        P("expert", "dp", None),
    )
    out_specs = (
        P(("groups", "expert", "dp"), None, None),
        P(("groups", "expert", "dp"), None),
        P(("groups", "expert"), "dp", None),
    )
    return jax.shard_map(
        on_device, mesh=mesh, in_specs=in_specs, out_specs=out_specs, check_vma=False
    )
```

profile of v0, /device:TPU:15, one launch (start us, length us, event | category | flops | bytes accessed | tf_op | source)
XLA Modules:
  0.0 340.9 jit_solution(6447728315691964159)
XLA Ops:
  0.7 0.8 broadcast_multiply_fusion
  1.5 0.8 copy.32
  2.5 0.8 copy.30
  3.6 4.5 %reduce-window.6 = s32[16,8,128]{2,1,0:T(8,128)S(1)} reduce-window(s32[16,8,128]{2,1,0:T(8,128)S(1)} %fusion.14, s32[]{:T(128)} %constant.16.clone.1), window={size=1x1x128 pad=0_0x0_0x127_0}, to_apply=%region_0.0 | reduce-window | flops 2080768 | bytes 131076 | tf_op jit(solution)/shard_map/reduce-window
  8.6 4.3 %scatter_custom_fusion = s32[2048]{0:T(1024)S(1)} fusion(s32[1024]{0:T(1024)S(1)} %bitcast.65, s32[1024]{0:T(1024)S(1)} %iota.11, s32[]{:T(128)} %constant.14.clone.1), kind=kCustom, calls=%fused_computation.40 | custom fusion | bytes 8196 | tf_op jit(solution)/shard_map/scatter | solution.py:24
  12.9 13.1 %gather_fusion = bf16[2048]{0:T(1024)(128)(2,1)S(1)} fusion(bf16[1025]{0:T(1024)(128)(2,1)S(1)} %pad_maximum_fusion, s32[2048]{0:T(1024)S(1)} %get-tuple-element.14), kind=kCustom, calls=%fused_computation | custom fusion | bytes 16384 | tf_op jit(solution)/shard_map/gather | solution.py:34
  26.0 0.6 copy.36
  26.6 6.6 %all-to-all-start = ((bf16[16,1,128]{2,1,0:T(2,128)(2,1)}), bf16[16,1,128]{2,1,0:T(2,128)(2,1)S(1)}, u32[]{:S(2)}, u32[]{:S(2)}) async-start(bf16[16,1,128]{2,1,0:T(2,128)(2,1)} %copy.36), calls=%async_computation | async-start | bytes 16384 | tf_op jit(solution)/shard_map/all_to_all | solution.py:40
  33.3 9.1 %gather_fusion.3 = bf16[2048,384]{1,0:T(8,128)(2,1)} fusion(bf16[1025,384]{1,0:T(8,128)(2,1)S(1)} %concatenate.11, s32[2048]{0:T(1024)S(1)} %get-tuple-element.14), kind=kCustom, calls=%fused_computation.3 | custom fusion | bytes 3153920 | tf_op jit(solution)/shard_map/gather | solution.py:33
  42.4 2.7 copy.37
  45.0 6.0 %all-to-all-start.3 = ((bf16[16,128,384]{1,2,0:T(8,128)(2,1)}), bf16[16,128,384]{1,2,0:T(8,128)(2,1)}, u32[]{:S(2)}, u32[]{:S(2)}) async-start(bf16[16,128,384]{1,2,0:T(8,128)(2,1)} %copy.37), calls=%async_computation.3 | async-start | bytes 3145728 | tf_op jit(solution)/shard_map/all_to_all | solution.py:39
  51.1 11.0 %gather_fusion.1 = bf16[2048,2048]{1,0:T(8,128)(2,1)} fusion(bf16[129,2048]{1,0:T(8,128)(2,1)S(1)} %concatenate.10, s32[2048]{0:T(1024)S(1)} %get-tuple-element.15), kind=kCustom, calls=%fused_computation.1 | custom fusion | bytes 16785408 | tf_op jit(solution)/shard_map/gather | solution.py:32
  62.2 25.2 %all-to-all-done.3 = bf16[16,128,384]{1,2,0:T(8,128)(2,1)} async-done(((bf16[16,128,384]{1,2,0:T(8,128)(2,1)}), bf16[16,128,384]{1,2,0:T(8,128)(2,1)}, u32[]{:S(2)}, u32[]{:S(2)}) %all-to-all-start.3) | async-done | bytes 1572896 | tf_op jit(solution)/shard_map/all_to_all | solution.py:39
  87.3 4.9 %all-to-all-start.1 = ((bf16[16,128,2048]{2,1,0:T(8,128)(2,1)}), bf16[16,128,2048]{2,1,0:T(8,128)(2,1)}, u32[]{:S(2)}, u32[]{:S(2)}) async-start(bf16[16,128,2048]{2,1,0:T(8,128)(2,1)} %bitcast.56), calls=%async_computation.1 | async-start | bytes 16777216 | tf_op jit(solution)/shard_map/all_to_all | solution.py:38
  92.3 3.1 copy.38
  95.3 179.3 %all-to-all-done.1 = bf16[16,128,2048]{2,1,0:T(8,128)(2,1)} async-done(((bf16[16,128,2048]{2,1,0:T(8,128)(2,1)}), bf16[16,128,2048]{2,1,0:T(8,128)(2,1)}, u32[]{:S(2)}, u32[]{:S(2)}) %all-to-all-start.1) | async-done | bytes 8388640 | tf_op jit(solution)/shard_map/all_to_all | solution.py:38
  274.6 10.3 %fusion.3 = (bf16[2048]{0:T(1024)(128)(2,1)S(1)}, bf16[2048,384]{1,0:T(8,128)(2,1)}) fusion(f32[16,128,384]{2,1,0:T(8,128)} %copy.38, f32[2048]{0:T(1024)S(1)} %bitcast.67, bf16[2048,2048]{1,0:T(8,128)(2,1)} %bitcast.7, bf16[1,384,2048]{2,1,0:T(8,128)(2,1)S(1)} %copy-done), kind=kOutput, calls=%fused_computation.11 | convolution fusion | flops 3224369152 | bytes 14692352 | tf_op jit(solution)/shard_map/dot_general | solution.py:45
  284.9 8.5 %all_to_all.30 = bf16[16,1,128]{2,1,0:T(2,128)(2,1)S(1)} all-to-all(bf16[16,1,128]{2,1,0:T(2,128)(2,1)S(1)} %copy.39), channel_id=1, replica_groups=mesh['groups'=2,'expert'=16,'dp'=1] {'expert'}, dimensions={0} | all-to-all | bytes 8192 | tf_op jit(solution)/shard_map/all_to_all | solution.py:62
  293.4 6.2 %all-to-all-start.2 = ((bf16[16,128,384]{2,1,0:T(8,128)(2,1)}), bf16[16,128,384]{2,1,0:T(8,128)(2,1)S(1)}, u32[]{:S(2)}, u32[]{:S(2)}) async-start(bf16[16,128,384]{2,1,0:T(8,128)(2,1)} %bitcast.58), calls=%async_computation.2 | async-start | bytes 3145728 | tf_op jit(solution)/shard_map/all_to_all | solution.py:55
  299.7 7.3 %fusion.6 = bf16[1,384,2048]{2,1,0:T(8,128)(2,1)} fusion(bf16[16,128,384]{1,2,0:T(8,128)(2,1)} %all-to-all-done.3, bf16[16,128,2048]{2,1,0:T(8,128)(2,1)} %all-to-all-done.1, bf16[16,128]{1,0:T(8,128)(2,1)S(1)} %bitcast.69), kind=kOutput, calls=%fused_computation.13 | convolution fusion | flops 3226206208 | bytes 11538432 | tf_op jit(solution)/shard_map/dot_general | solution.py:71
  307.0 6.8 %gather_fusion.4 = bf16[1024]{0:T(1024)(128)(2,1)S(1)} fusion(bf16[2048]{0:T(1024)(128)(2,1)S(1)} %bitcast.54, s32[1024]{0:T(1024)S(1)} %broadcast_clamp_fusion), kind=kCustom, calls=%fused_computation.4 | custom fusion | bytes 8192 | tf_op jit(solution)/shard_map/gather | solution.py:82
  313.9 0.7 copy.40
  314.6 21.3 %all-to-all-done.2 = bf16[16,128,384]{2,1,0:T(8,128)(2,1)S(1)} async-done(((bf16[16,128,384]{2,1,0:T(8,128)(2,1)}), bf16[16,128,384]{2,1,0:T(8,128)(2,1)S(1)}, u32[]{:S(2)}, u32[]{:S(2)}) %all-to-all-start.2) | async-done | bytes 1572896 | tf_op jit(solution)/shard_map/all_to_all | solution.py:55
  335.9 5.0 %gather_fusion.2 = bf16[1024,384]{1,0:T(8,128)(2,1)} fusion(bf16[2048,384]{1,0:T(8,128)(2,1)S(1)} %bitcast.55, s32[1024]{0:T(1024)S(1)} %broadcast_clamp_fusion), kind=kCustom, calls=%fused_computation.2 | custom fusion | bytes 1576960 | tf_op jit(solution)/shard_map/gather | solution.py:79
  (32 shorter events, 1.3 us)
Async XLA Ops:
  0.6 274.0 %copy-start = (bf16[1,384,2048]{2,1,0:T(8,128)(2,1)S(1)}, bf16[1,384,2048]{2,1,0:T(8,128)(2,1)}, u32[]{:S(2)}) copy-start(bf16[1,384,2048]{2,1,0:T(8,128)(2,1)} %param.9) | copy-start | bytes 4718596
  0.6 32.6 %copy-start.1 = (bf16[128,8,384]{2,1,0:T(8,128)(2,1)S(1)}, bf16[128,8,384]{2,1,0:T(8,128)(2,1)}, u32[]{:S(2)}) copy-start(bf16[128,8,384]{2,1,0:T(8,128)(2,1)} %param.6) | copy-start | bytes 2359300
  26.6 18.4 %all-to-all-start = ((bf16[16,1,128]{2,1,0:T(2,128)(2,1)}), bf16[16,1,128]{2,1,0:T(2,128)(2,1)S(1)}, u32[]{:S(2)}, u32[]{:S(2)}) async-start(bf16[16,1,128]{2,1,0:T(2,128)(2,1)} %copy.36), calls=%async_computation | async-start | bytes 16384 | tf_op jit(solution)/shard_map/all_to_all | solution.py:40
  42.4 8.7 %copy-start.2 = (bf16[128,2048]{1,0:T(8,128)(2,1)S(1)}, bf16[128,2048]{1,0:T(8,128)(2,1)}, u32[]{:S(2)}) copy-start(bf16[128,2048]{1,0:T(8,128)(2,1)} %param.5) | copy-start | bytes 1572868
  45.0 42.3 %all-to-all-start.3 = ((bf16[16,128,384]{1,2,0:T(8,128)(2,1)}), bf16[16,128,384]{1,2,0:T(8,128)(2,1)}, u32[]{:S(2)}, u32[]{:S(2)}) async-start(bf16[16,128,384]{1,2,0:T(8,128)(2,1)} %copy.37), calls=%async_computation.3 | async-start | bytes 3145728 | tf_op jit(solution)/shard_map/all_to_all | solution.py:39
  87.3 187.3 %all-to-all-start.1 = ((bf16[16,128,2048]{2,1,0:T(8,128)(2,1)}), bf16[16,128,2048]{2,1,0:T(8,128)(2,1)}, u32[]{:S(2)}, u32[]{:S(2)}) async-start(bf16[16,128,2048]{2,1,0:T(8,128)(2,1)} %bitcast.56), calls=%async_computation.1 | async-start | bytes 16777216 | tf_op jit(solution)/shard_map/all_to_all | solution.py:38
  293.4 42.4 %all-to-all-start.2 = ((bf16[16,128,384]{2,1,0:T(8,128)(2,1)}), bf16[16,128,384]{2,1,0:T(8,128)(2,1)S(1)}, u32[]{:S(2)}, u32[]{:S(2)}) async-start(bf16[16,128,384]{2,1,0:T(8,128)(2,1)} %bitcast.58), calls=%async_computation.2 | async-start | bytes 3145728 | tf_op jit(solution)/shard_map/all_to_all | solution.py:55
where the time goes:
time: 341 us
  waiting for transfers between devices  226 us (66%)
  local copies, waits for them, and re-layouts  58.9 us (17%)
  starting transfers between devices  23.7 us (7%)
  matrix products  17.6 us (5%)
  blocking collectives  8.51 us (2%)
  other arithmetic  5.59 us (2%)
    all_to_all x1, waiting for transfers between devices, on_device(): lax.all_to_all(send_grad, 'expert', split_axis=0, concat_axis=0, tiled=True)  179 us
    all_to_all x1, waiting for transfers between devices, on_device(): lax.all_to_all(send_hidden, 'expert', split_axis=0, concat_axis=0, tiled=...  25.2 us
    all_to_all x1, waiting for transfers between devices, on_device(): lax.all_to_all(hidden_grads.reshape(peer_count, capacity, inner_width), '...  21.3 us
    gather x1, local copies, waits for them, and re-layouts, on_device(): send_probs = probs_ext[slot_table].reshape(peer_count, capacity)  13.1 us
    gather x1, local copies, waits for them, and re-layouts, on_device(): send_grad = grad_ext[token_index].reshape(peer_count, capacity, model_width)  11 us
    dot_general x1, matrix products, on_device(): lax.dot_general(grad_rows, lax.all_gather(local_weight, 'dp', axis=0, til...  10.3 us
    gather x1, local copies, waits for them, and re-layouts, on_device(): hidden_ext[slot_table].reshape(peer_count, capacity, inner_width)  9.09 us
    all_to_all x1, blocking collectives, on_device(): lax.all_to_all(prob_grads.reshape(peer_count, capacity), 'expert', split_...  8.51 us
  transfers between devices with their start and end apart: 4, of which 3 were waited for; matrix products, arithmetic and copies ran while one was open for 12% of the time, Pallas kernels for 0%

commit v1 on v0

--- a/solution.py
+++ b/solution.py
@@ -1,10 +1,18 @@
+import functools
+
 import jax
 import jax.numpy as jnp
+import numpy as np
 from jax import lax
+from jax.experimental import pallas as pl
+from jax.experimental.pallas import tpu as pltpu
 from jax.sharding import PartitionSpec as P
 
-
-def on_device(grad_out, hidden, routes, probs, w_down):
+GROUP = 16
+VMEM = 48 * 1024 * 1024
+
+
+def padded_on_device(grad_out, hidden, routes, probs, w_down):
     token_count, model_width = grad_out.shape
     top_count = routes.shape[1]
     inner_width = hidden.shape[2]
@@ -83,6 +91,250 @@
     return (grad_hidden, grad_probs, grad_w)
 
 
+def chosen_slots(route_row, expert_count, top_count):
+    shape = (expert_count * GROUP, GROUP * top_count)
+    row = lax.broadcasted_iota(jnp.int32, shape, 0)
+    col = lax.broadcasted_iota(jnp.int32, shape, 1)
+    return (row % GROUP == col // top_count) & (row // GROUP == route_row)
+
+
+def dispatch_kernel(routes_ref, probs_ref, hidden_ref, out_ref, *, expert_count, top_count):
+    span = GROUP * top_count
+    inner_width = hidden_ref.shape[1]
+    for g in range(routes_ref.shape[0]):
+        chosen = chosen_slots(routes_ref[g : g + 1, :], expert_count, top_count)
+        pick = jnp.where(chosen, probs_ref[g : g + 1, :].astype(jnp.float32), 0.0)
+        rows = jnp.dot(
+            pick.astype(jnp.bfloat16),
+            hidden_ref[g * span : (g + 1) * span, :],
+            preferred_element_type=jnp.float32,
+        ).astype(jnp.bfloat16)
+        out_ref[:, g * GROUP : (g + 1) * GROUP, :] = rows.reshape(expert_count, GROUP, inner_width)
+
+
+def combine_kernel(
+    routes_ref, probs_ref, hidden_ref, back_ref, hid_ref, prob_ref, *, expert_count, top_count
+):
+    span = GROUP * top_count
+    inner_width = hidden_ref.shape[1]
+    ones = jnp.ones((8, inner_width), jnp.bfloat16)
+    across = (((0,), (0,)), ((), ()))
+    lanes = (((1,), (1,)), ((), ()))
+    for g in range(routes_ref.shape[0]):
+        chosen = chosen_slots(routes_ref[g : g + 1, :], expert_count, top_count)
+        pick = jnp.where(chosen, 1.0, 0.0).astype(jnp.bfloat16)
+        scaled = jnp.where(chosen, probs_ref[g : g + 1, :].astype(jnp.float32), 0.0)
+        block = back_ref[:, g * GROUP : (g + 1) * GROUP, :].reshape(expert_count * GROUP, inner_width)
+        mine = lax.dot_general(pick, block, across, preferred_element_type=jnp.float32)
+        hid_ref[g * span : (g + 1) * span, :] = lax.dot_general(
+            scaled.astype(jnp.bfloat16), block, across, preferred_element_type=jnp.float32
+        ).astype(jnp.bfloat16)
+        product = mine * hidden_ref[g * span : (g + 1) * span, :].astype(jnp.float32)
+        high = product.astype(jnp.bfloat16)
+        low = (product - high.astype(jnp.float32)).astype(jnp.bfloat16)
+        total = lax.dot_general(ones, high, lanes, preferred_element_type=jnp.float32)
+        total += lax.dot_general(ones, low, lanes, preferred_element_type=jnp.float32)
+        prob_ref[g : g + 1, :] = total[0:1, :].astype(jnp.bfloat16)
+
+
+def back_kernel(ids_ref, *refs, places, step):
+    pieces, (w_ref, out_ref, held, sems) = refs[: len(places)], refs[len(places) :]
+    copies = []
+    for i, (first, rows) in enumerate(places):
+        copies.append(
+            pltpu.make_async_copy(pieces[i], held.at[pl.ds(first, rows)], sems.at[i])
+        )
+        copies[i].start()
+    block = out_ref.shape[1]
+    waited = 0
+    for first in range(0, held.shape[0], step):
+        while waited < len(places) and places[waited][0] < first + step:
+            copies[waited].wait()
+            waited += 1
+        rows = lax.dot_general(
+            held[first : first + step, :],
+            w_ref[...],
+            (((1,), (1,)), ((), ())),
+            preferred_element_type=jnp.float32,
+        ).astype(jnp.bfloat16)
+        for j in range(step // block):
+            out_ref[ids_ref[first // block + j]] = rows[j * block : (j + 1) * block, :]
+
+
+def weight_kernel(ids_ref, *refs, places, tile):
+    pieces, (hidden_ref, out_ref, held, rows_held, sems, row_sems) = (
+        refs[: len(places)],
+        refs[len(places) :],
+    )
+    block = hidden_ref.shape[1]
+    copies = []
+    for j in range(hidden_ref.shape[0]):
+        copies.append(
+            pltpu.make_async_copy(
+                hidden_ref.at[ids_ref[j]], rows_held.at[pl.ds(j * block, block)], row_sems.at[j]
+            )
+        )
+    for i, (first, rows) in enumerate(places):
+        copies.append(
+            pltpu.make_async_copy(pieces[i], held.at[pl.ds(first, rows)], sems.at[i])
+        )
+    for copy in copies:
+        copy.start()
+    for copy in copies:
+        copy.wait()
+
+    @pl.loop(0, out_ref.shape[1] // tile)
+    def _(n):
+        cols = pl.ds(pl.multiple_of(n * tile, tile), tile)
+        out_ref[:, cols] = lax.dot_general(
+            rows_held[...],
+            held[:, cols],
+            (((0,), (0,)), ((), ())),
+            preferred_element_type=jnp.float32,
+        ).astype(jnp.bfloat16)
+
+
+def ring_of_chips(chip_count):
+    return list(range(0, chip_count, 2)) + list(range(chip_count - 1, 0, -2))
+
+
+def gather_round(grad_out, peer_count):
+    token_count = grad_out.shape[0]
+    half = token_count // 2
+    chips = peer_count // 2
+    ring = ring_of_chips(chips)
+    place = {chip: i for i, chip in enumerate(ring)}
+    ahead = [
+        (2 * chip + core, 2 * ring[(place[chip] + 1) % chips] + core)
+        for chip in range(chips)
+        for core in range(2)
+    ]
+    behind = [(b, a) for a, b in ahead]
+    swap = [(i, i ^ 1) for i in range(peer_count)]
+    offsets, own_core = [0], []
+    own_core.append([(grad_out, 0, token_count)])
+    fore = aft = grad_out
+    for s in range(1, chips // 2):
+        fore = lax.ppermute(fore, "expert", ahead)
+        aft = lax.ppermute(aft, "expert", behind)
+        own_core += [[(fore, 0, token_count)], [(aft, 0, token_count)]]
+        offsets += [-s, s]
+    own_core.append(
+        [
+            (lax.ppermute(fore[:half], "expert", ahead), 0, half),
+            (lax.ppermute(aft[half:], "expert", behind), half, half),
+        ]
+    )
+    offsets.append(chips // 2)
+    pieces, places = [], []
+    table = np.zeros((peer_count, peer_count), np.int32)
+    for i, parts in enumerate(own_core):
+        for j in range(2):
+            for array, first, rows in parts:
+                pieces.append(lax.ppermute(array, "expert", swap) if j else array)
+                places.append(((2 * i + j) * token_count + first, rows))
+        for peer in range(peer_count):
+            chip, core = peer // 2, peer % 2
+            source = ring[(place[chip] + offsets[i]) % chips]
+            table[peer, 2 * i] = 2 * source + core
+            table[peer, 2 * i + 1] = 2 * source + 1 - core
+    ids = lax.dynamic_index_in_dim(
+        jnp.asarray(table), lax.axis_index("expert"), 0, keepdims=False
+    )
+    return pieces, places, ids
+
+
+def dense_on_device(grad_out, hidden, routes, probs, w_down):
+    token_count, model_width = grad_out.shape
+    top_count = routes.shape[1]
+    inner_width = hidden.shape[2]
+    peer_count = lax.axis_size("expert")
+    slot_count = token_count * top_count
+    row_count = peer_count * token_count
+    span = GROUP * top_count
+    route_rows = routes.reshape(slot_count // span, span)
+    prob_rows = probs.reshape(slot_count // span, span)
+    hidden_rows = hidden.reshape(slot_count, inner_width)
+    local_weight = w_down[0]
+    sizes = dict(expert_count=peer_count, top_count=top_count)
+    params = pltpu.CompilerParams(vmem_limit_bytes=VMEM)
+    anywhere = pl.BlockSpec(memory_space=pl.ANY)
+    whole = pl.BlockSpec(memory_space=pltpu.VMEM)
+
+    pieces, places, ids = gather_round(grad_out, peer_count)
+
+    sent_hidden = pl.pallas_call(
+        functools.partial(dispatch_kernel, **sizes),
+        out_shape=jax.ShapeDtypeStruct((peer_count, token_count, inner_width), jnp.bfloat16),
+        in_specs=[whole] * 3,
+        out_specs=whole,
+        compiler_params=params,
+        name="dispatch",
+    )(route_rows, prob_rows, hidden_rows)
+    got_hidden = lax.all_to_all(sent_hidden, "expert", split_axis=0, concat_axis=0, tiled=True)
+
+    back = pl.pallas_call(
+        functools.partial(back_kernel, places=places, step=4 * token_count),
+        out_shape=jax.ShapeDtypeStruct((peer_count, token_count, inner_width), jnp.bfloat16),
+        in_specs=[pl.BlockSpec(memory_space=pltpu.SMEM)] + [anywhere] * len(pieces) + [whole],
+        out_specs=whole,
+        scratch_shapes=[
+            pltpu.VMEM((row_count, model_width), jnp.bfloat16),
+            pltpu.SemaphoreType.DMA((len(pieces),)),
+        ],
+        compiler_params=params,
+        name="back_rows",
+    )(ids, *pieces, local_weight)
+    got_back = lax.all_to_all(back, "expert", split_axis=0, concat_axis=0, tiled=True)
+
+    grad_w = pl.pallas_call(
+        functools.partial(weight_kernel, places=places, tile=512),
+        out_shape=jax.ShapeDtypeStruct((inner_width, model_width), jnp.bfloat16),
+        in_specs=[pl.BlockSpec(memory_space=pltpu.SMEM)] + [anywhere] * (len(pieces) + 1),
+        out_specs=whole,
+        scratch_shapes=[
+            pltpu.VMEM((row_count, model_width), jnp.bfloat16),
+            pltpu.VMEM((row_count, inner_width), jnp.bfloat16),
+            pltpu.SemaphoreType.DMA((len(pieces),)),
+            pltpu.SemaphoreType.DMA((peer_count,)),
+        ],
+        compiler_params=params,
+        name="grad_w",
+    )(ids, *pieces, got_hidden)
+
+    grad_hidden, grad_probs = pl.pallas_call(
+        functools.partial(combine_kernel, **sizes),
+        out_shape=(
+            jax.ShapeDtypeStruct((slot_count, inner_width), jnp.bfloat16),
+            jax.ShapeDtypeStruct((slot_count // span, span), jnp.bfloat16),
+        ),
+        in_specs=[whole] * 4,
+        out_specs=(whole, whole),
+        compiler_params=params,
+        name="combine",
+    )(route_rows, prob_rows, hidden_rows, got_back)
+    return (
+        grad_hidden.reshape(token_count, top_count, inner_width),
+        grad_probs.reshape(token_count, top_count),
+        grad_w[None],
+    )
+
+
+def on_device(grad_out, hidden, routes, probs, w_down):
+    token_count = grad_out.shape[0]
+    top_count = routes.shape[1]
+    peer_count = lax.axis_size("expert")
+    dense = (
+        2 * top_count >= peer_count
+        and lax.axis_size("dp") == 1
+        and peer_count % 4 == 0
+        and token_count % (2 * GROUP) == 0
+        and (GROUP * top_count) % 128 == 0
+    )
+    body = dense_on_device if dense else padded_on_device
+    return body(grad_out, hidden, routes, probs, w_down)
+
+
 def solution(mesh):
     in_specs = (
         P(("groups", "expert", "dp"), None),

time: 341 us -> 157 us (0.46)
  waiting for transfers between devices: 226 us -> 87 us
  local copies, waits for them, and re-layouts: 58.9 us -> 20.1 us
  Pallas kernels: 0 us -> 20.7 us
  matrix products: 17.6 us -> 0 us
  blocking collectives: 8.51 us -> 0 us
  other arithmetic: 5.59 us -> 0 us
    all_to_all x4 -> x2, waiting for transfers between devices: 226 us -> 19.3 us  [the longest x1 19.3 us: dense_on_device(): lax.all_to_all(back, 'expert', split_axis=0, concat_axis=0, tiled=True)]
    ppermute x0 -> x17, waiting for transfers between devices: none -> 67.7 us  [the longest x3 64.3 us: gather_round(): fore = lax.ppermute(fore, 'expert', ahead)]
    gather x5 -> x0, local copies, waits for them, and re-layouts: 45 us -> none  [the longest x1 13.1 us: on_device(): send_probs = probs_ext[slot_table].reshape(peer_count, capacity)]
    pallas_call x0 -> x4, Pallas kernels: none -> 20.7 us  [the longest x1 8.6 us: dense_on_device(): pl.pallas_call(functools.partial(weight_kernel, places=places, tile=512),...]
    dot_general x2 -> x0, matrix products: 17.6 us -> none  [the longest x1 10.3 us: on_device(): lax.dot_general(grad_rows, lax.all_gather(local_weight, 'dp', axis=0, til...]
    ppermute x0 -> x17, starting transfers between devices: none -> 15.1 us  [the longest x9 9.12 us: gather_round(): pieces.append(lax.ppermute(array, 'expert', swap) if j else array)]
    unnamed x10 -> x47, local copies, waits for them, and re-layouts: 2.27 us -> 17.2 us
    all_to_all x4 -> x2, starting transfers between devices: 23.7 us -> 11.9 us  [the longest x1 6.71 us: dense_on_device(): lax.all_to_all(sent_hidden, 'expert', split_axis=0, concat_axis=0, tiled=...]
  transfers between devices with their start and end apart: 4 -> 19, of which waited for: 3 -> 6; matrix products, arithmetic and copies ran while one was open for 12% -> 2% of each run, Pallas kernels for 0% -> 11%
where the time goes in v1:
time: 157 us; the launch traced here: 156 us
  waiting for transfers between devices  87 us (55%)
  starting transfers between devices  27 us (17%)
  Pallas kernels  20.7 us (13%)
  local copies, waits for them, and re-layouts  20.1 us (13%)
    ppermute x3, waiting for transfers between devices, gather_round(): fore = lax.ppermute(fore, 'expert', ahead)  64.3 us
    all_to_all x1, waiting for transfers between devices, dense_on_device(): lax.all_to_all(back, 'expert', split_axis=0, concat_axis=0, tiled=True)  19.3 us
    unnamed x47, local copies, waits for them, and re-layouts  17.2 us
    ppermute x9, starting transfers between devices, gather_round(): pieces.append(lax.ppermute(array, 'expert', swap) if j else array)  9.12 us
    pallas_call x1, Pallas kernels, dense_on_device(): pl.pallas_call(functools.partial(weight_kernel, places=places, tile=512),...  8.6 us
    pallas_call x1, Pallas kernels, dense_on_device(): pl.pallas_call(functools.partial(back_kernel, places=places, step=4 * tok...  8.22 us
    all_to_all x1, starting transfers between devices, dense_on_device(): lax.all_to_all(sent_hidden, 'expert', split_axis=0, concat_axis=0, tiled=...  6.71 us
    all_to_all x1, starting transfers between devices, dense_on_device(): lax.all_to_all(back, 'expert', split_axis=0, concat_axis=0, tiled=True)  5.22 us
  transfers between devices with their start and end apart: 19, of which 6 were waited for; matrix products, arithmetic and copies ran while one was open for 2% of the time, Pallas kernels for 11%

profile of v1, /device:TPU:15, one launch (start us, length us, event | category | flops | bytes accessed | tf_op | source)
XLA Modules:
  0.0 155.7 jit_solution(5692351595115785606)
XLA Ops:
  2.4 1.1 copy-done
  3.6 1.7 %dispatch.1 = bf16[16,128,384]{2,1,0:T(8,128)(2,1)} custom-call(s32[8,128]{1,0:T(8,128)S(1)} %reshape.21.routes_ref, bf16[8,128]{1,0:T(8,128)(2,1)S(1)} %reshape.22.probs_ref, bf16[1024,384]{1,0:T(8,128)(2,1)S(1)} %bitcast.6), custom_call_target="tpu_custom_call" | custom-call | tf_op jit(solution)/shard_map/dispatch/pallas_call | solution.py:266
  5.3 6.7 %all-to-all-start.1 = ((bf16[16,128,384]{2,1,0:T(8,128)(2,1)}), bf16[16,128,384]{2,1,0:T(8,128)(2,1)}, u32[]{:S(2)}, u32[]{:S(2)}) async-start(bf16[16,128,384]{2,1,0:T(8,128)(2,1)} %dispatch.1), calls=%async_computation.1 | async-start | bytes 3145728 | tf_op jit(solution)/shard_map/all_to_all | solution.py:274
  12.3 1.2 collective-permute-start.3
  13.5 45.8 %collective-permute-done.1.refs_2_ = bf16[128,2048]{1,0:T(8,128)(2,1)S(1)} collective-permute-done((bf16[128,2048]{1,0:T(8,128)(2,1)S(1)}, bf16[128,2048]{1,0:T(8,128)(2,1)S(1)}, u32[]{:S(2)}, u32[]{:S(2)}) %collective-permute-start.1) | collective-permute-done | bytes 524320 | tf_op jit(solution)/shard_map/ppermute | solution.py:218
  59.3 1.5 collective-permute-start.7
  60.8 11.1 %collective-permute-done.5.refs_6_ = bf16[128,2048]{1,0:T(8,128)(2,1)S(1)} collective-permute-done((bf16[128,2048]{1,0:T(8,128)(2,1)S(1)}, bf16[128,2048]{1,0:T(8,128)(2,1)S(1)}, u32[]{:S(2)}, u32[]{:S(2)}) %collective-permute-start.5) | collective-permute-done | bytes 524320 | tf_op jit(solution)/shard_map/ppermute | solution.py:218
  72.2 1.1 collective-permute-start.11
  73.3 2.3 %collective-permute-start = (bf16[128,2048]{1,0:T(8,128)(2,1)S(1)}, bf16[128,2048]{1,0:T(8,128)(2,1)S(1)}, u32[]{:S(2)}, u32[]{:S(2)}) collective-permute-start(bf16[128,2048]{1,0:T(8,128)(2,1)S(1)} %copy-done.2), channel_id=1, source_target_pairs={{0,1},{1,0},{2,3},{3,2},{4,5},{5,4},{6,7},{7,6},{8,9},{9,8},{10,11... | collective-permute-start | bytes 1572872 | tf_op jit(solution)/shard_map/ppermute | solution.py:234
  76.2 7.4 %collective-permute-done.9.refs_10_ = bf16[128,2048]{1,0:T(8,128)(2,1)} collective-permute-done((bf16[128,2048]{1,0:T(8,128)(2,1)S(1)}, bf16[128,2048]{1,0:T(8,128)(2,1)}, u32[]{:S(2)}, u32[]{:S(2)}) %collective-permute-start.9) | collective-permute-done | bytes 524320 | tf_op jit(solution)/shard_map/ppermute | solution.py:218
  83.6 2.7 %collective-permute-start.6 = (bf16[128,2048]{1,0:T(8,128)(2,1)S(1)}, bf16[128,2048]{1,0:T(8,128)(2,1)S(1)}, u32[]{:S(2)}, u32[]{:S(2)}) collective-permute-start(bf16[128,2048]{1,0:T(8,128)(2,1)S(1)} %collective-permute-done.5.refs_6_), channel_id=1, source_target_pairs={{0,1},{1,0},{2,3},{3,2},{4,5},{5,4},{6,7},{7,6},{8,9},{9,8},{10,11... | collective-permute-start | bytes 1572872 | tf_op jit(solution)/shard_map/ppermute | solution.py:234
  89.5 1.1 collective-permute-start.14
  91.5 1.1 collective-permute-start.10
  93.4 2.5 %collective-permute-done.13.refs_14_ = bf16[64,2048]{1,0:T(8,128)(2,1)S(1)} collective-permute-done((bf16[64,2048]{1,0:T(8,128)(2,1)S(1)}, bf16[64,2048]{1,0:T(8,128)(2,1)S(1)}, u32[]{:S(2)}, u32[]{:S(2)}) %collective-permute-start.13) | collective-permute-done | bytes 262176 | tf_op jit(solution)/shard_map/ppermute | solution.py:224
  95.9 1.2 collective-permute-start.15
  97.1 1.2 collective-permute-start.16
  99.9 1.0 copy-done.12
  102.0 1.0 copy-done.18
  103.0 8.2 %back_rows.1 = bf16[16,128,384]{2,1,0:T(8,128)(2,1)} custom-call(s32[16]{0:T(128)S(1)} %dynamic-slice_bitcast_fusion.ids_ref, bf16[128,2048]{1,0:T(8,128)(2,1)S(1)} %copy-done.2, bf16[128,2048]{1,0:T(8,128)(2,1)S(1)} %collective-permute-done.refs_1_, bf16[128,2048]{1,0:T(8,128)(2,1)S(1)} %collective-permute-done.1.refs_2_, bf16[128,2048]{1,0:T(8,128)(2,1)S(1)} %copy-done.12, ...), custom_call_target="tpu_custom_call" | custom-call | tf_op jit(solution)/shard_map/back_rows/pallas_call | solution.py:276
  111.3 5.2 %all-to-all-start = ((bf16[16,128,384]{2,1,0:T(8,128)(2,1)}), bf16[16,128,384]{2,1,0:T(8,128)(2,1)S(1)}, u32[]{:S(2)}, u32[]{:S(2)}) async-start(bf16[16,128,384]{2,1,0:T(8,128)(2,1)} %back_rows.1), calls=%async_computation | async-start | bytes 3145728 | tf_op jit(solution)/shard_map/all_to_all | solution.py:288
  117.6 1.0 copy-done.6
  124.8 8.6 %grad_w.1 = bf16[384,2048]{1,0:T(8,128)(2,1)} custom-call(s32[16]{0:T(128)S(1)} %dynamic-slice_bitcast_fusion.ids_ref, bf16[128,2048]{1,0:T(8,128)(2,1)S(1)} %copy-done.2, bf16[128,2048]{1,0:T(8,128)(2,1)S(1)} %copy-done.10, bf16[128,2048]{1,0:T(8,128)(2,1)S(1)} %collective-permute-done.1.refs_2_, bf16[128,2048]{1,0:T(8,128)(2,1)S(1)} %copy-done.13, ...), custom_call_target="tpu_custom_call" | custom-call | tf_op jit(solution)/shard_map/grad_w/pallas_call | solution.py:290
  133.4 19.3 %all-to-all-done.back_ref = bf16[16,128,384]{2,1,0:T(8,128)(2,1)S(1)} async-done(((bf16[16,128,384]{2,1,0:T(8,128)(2,1)}), bf16[16,128,384]{2,1,0:T(8,128)(2,1)S(1)}, u32[]{:S(2)}, u32[]{:S(2)}) %all-to-all-start) | async-done | bytes 1572896 | tf_op jit(solution)/shard_map/all_to_all | solution.py:288
  152.7 2.2 %combine.1 = (bf16[1024,384]{1,0:T(8,128)(2,1)}, bf16[8,128]{1,0:T(8,128)(2,1)S(1)}) custom-call(s32[8,128]{1,0:T(8,128)S(1)} %reshape.21.routes_ref, bf16[8,128]{1,0:T(8,128)(2,1)S(1)} %reshape.22.probs_ref, bf16[1024,384]{1,0:T(8,128)(2,1)S(1)} %bitcast.7, bf16[16,128,384]{2,1,0:T(8,128)(2,1)S(1)} %all-to-all-done.back_ref), custom_call_target="tpu_custom_call" | custom-call | tf_op jit(solution)/shard_map/combine/pallas_call | solution.py:305
  (71 shorter events, 18.3 us)
Async XLA Ops:
  5.3 106.0 %all-to-all-start.1 = ((bf16[16,128,384]{2,1,0:T(8,128)(2,1)}), bf16[16,128,384]{2,1,0:T(8,128)(2,1)}, u32[]{:S(2)}, u32[]{:S(2)}) async-start(bf16[16,128,384]{2,1,0:T(8,128)(2,1)} %dispatch.1), calls=%async_computation.1 | async-start | bytes 3145728 | tf_op jit(solution)/shard_map/all_to_all | solution.py:274
  12.0 47.3 %collective-permute-start.1 = (bf16[128,2048]{1,0:T(8,128)(2,1)S(1)}, bf16[128,2048]{1,0:T(8,128)(2,1)S(1)}, u32[]{:S(2)}, u32[]{:S(2)}) collective-permute-start(bf16[128,2048]{1,0:T(8,128)(2,1)S(1)} %copy-done.2), channel_id=1, source_target_pairs={{0,4},{1,5},{2,0},{3,1},{4,8},{5,9},{6,2},{7,3},{8,12},{9,13},{10,... | collective-permute-start | bytes 1572872 | tf_op jit(solution)/shard_map/ppermute | solution.py:218
  12.3 47.0 %collective-permute-start.3 = (bf16[128,2048]{1,0:T(8,128)(2,1)S(1)}, bf16[128,2048]{1,0:T(8,128)(2,1)S(1)}, u32[]{:S(2)}, u32[]{:S(2)}) collective-permute-start(bf16[128,2048]{1,0:T(8,128)(2,1)S(1)} %copy-done.2), channel_id=1, source_target_pairs={{4,0},{5,1},{0,2},{1,3},{8,4},{9,5},{2,6},{3,7},{12,8},{13,9},{6,1... | collective-permute-start | bytes 1572872 | tf_op jit(solution)/shard_map/ppermute | solution.py:219
  59.3 12.6 %collective-permute-start.5 = (bf16[128,2048]{1,0:T(8,128)(2,1)S(1)}, bf16[128,2048]{1,0:T(8,128)(2,1)S(1)}, u32[]{:S(2)}, u32[]{:S(2)}) collective-permute-start(bf16[128,2048]{1,0:T(8,128)(2,1)S(1)} %collective-permute-done.1.refs_2_), channel_id=1, source_target_pairs={{0,4},{1,5},{2,0},{3,1},{4,8},{5,9},{6,2},{7,3},{8,12},{9,13},{10,... | collective-permute-start | bytes 1572872 | tf_op jit(solution)/shard_map/ppermute | solution.py:218
  59.3 51.9 %copy-start.3 = (bf16[128,2048]{1,0:T(8,128)(2,1)}, bf16[128,2048]{1,0:T(8,128)(2,1)S(1)}, u32[]{:S(2)}) copy-start(bf16[128,2048]{1,0:T(8,128)(2,1)S(1)} %collective-permute-done.3.refs_4_) | copy-start | bytes 1572868
  59.3 12.9 %collective-permute-start.7 = (bf16[128,2048]{1,0:T(8,128)(2,1)S(1)}, bf16[128,2048]{1,0:T(8,128)(2,1)S(1)}, u32[]{:S(2)}, u32[]{:S(2)}) collective-permute-start(bf16[128,2048]{1,0:T(8,128)(2,1)S(1)} %collective-permute-done.3.refs_4_), channel_id=1, source_target_pairs={{4,0},{5,1},{0,2},{1,3},{8,4},{9,5},{2,6},{3,7},{12,8},{13,9},{6,1... | collective-permute-start | bytes 1572872 | tf_op jit(solution)/shard_map/ppermute | solution.py:219
  71.9 39.4 %copy-start.5 = (bf16[128,2048]{1,0:T(8,128)(2,1)}, bf16[128,2048]{1,0:T(8,128)(2,1)S(1)}, u32[]{:S(2)}) copy-start(bf16[128,2048]{1,0:T(8,128)(2,1)S(1)} %collective-permute-done.5.refs_6_) | copy-start | bytes 1572868
  71.9 11.8 %collective-permute-start.9 = (bf16[128,2048]{1,0:T(8,128)(2,1)S(1)}, bf16[128,2048]{1,0:T(8,128)(2,1)}, u32[]{:S(2)}, u32[]{:S(2)}) collective-permute-start(bf16[128,2048]{1,0:T(8,128)(2,1)S(1)} %collective-permute-done.5.refs_6_), channel_id=1, source_target_pairs={{0,4},{1,5},{2,0},{3,1},{4,8},{5,9},{6,2},{7,3},{8,12},{9,13},{10,... | collective-permute-start | bytes 1572872 | tf_op jit(solution)/shard_map/ppermute | solution.py:218
  72.2 39.1 %copy-start.7 = (bf16[128,2048]{1,0:T(8,128)(2,1)}, bf16[128,2048]{1,0:T(8,128)(2,1)S(1)}, u32[]{:S(2)}) copy-start(bf16[128,2048]{1,0:T(8,128)(2,1)S(1)} %collective-permute-done.7.refs_8_) | copy-start | bytes 1572868
  72.2 15.1 %collective-permute-start.11 = (bf16[128,2048]{1,0:T(8,128)(2,1)S(1)}, bf16[128,2048]{1,0:T(8,128)(2,1)}, u32[]{:S(2)}, u32[]{:S(2)}) collective-permute-start(bf16[128,2048]{1,0:T(8,128)(2,1)S(1)} %collective-permute-done.7.refs_8_), channel_id=1, source_target_pairs={{4,0},{5,1},{0,2},{1,3},{8,4},{9,5},{2,6},{3,7},{12,8},{13,9},{6,1... | collective-permute-start | bytes 1572872 | tf_op jit(solution)/shard_map/ppermute | solution.py:219
  73.3 15.0 %collective-permute-start = (bf16[128,2048]{1,0:T(8,128)(2,1)S(1)}, bf16[128,2048]{1,0:T(8,128)(2,1)S(1)}, u32[]{:S(2)}, u32[]{:S(2)}) collective-permute-start(bf16[128,2048]{1,0:T(8,128)(2,1)S(1)} %copy-done.2), channel_id=1, source_target_pairs={{0,1},{1,0},{2,3},{3,2},{4,5},{5,4},{6,7},{7,6},{8,9},{9,8},{10,11... | collective-permute-start | bytes 1572872 | tf_op jit(solution)/shard_map/ppermute | solution.py:234
  75.7 13.1 %collective-permute-start.2 = (bf16[128,2048]{1,0:T(8,128)(2,1)S(1)}, bf16[128,2048]{1,0:T(8,128)(2,1)S(1)}, u32[]{:S(2)}, u32[]{:S(2)}) collective-permute-start(bf16[128,2048]{1,0:T(8,128)(2,1)S(1)} %collective-permute-done.1.refs_2_), channel_id=1, source_target_pairs={{0,1},{1,0},{2,3},{3,2},{4,5},{5,4},{6,7},{7,6},{8,9},{9,8},{10,11... | collective-permute-start | bytes 1572872 | tf_op jit(solution)/shard_map/ppermute | solution.py:234
  75.7 15.0 %collective-permute-start.4 = (bf16[128,2048]{1,0:T(8,128)(2,1)S(1)}, bf16[128,2048]{1,0:T(8,128)(2,1)S(1)}, u32[]{:S(2)}, u32[]{:S(2)}) collective-permute-start(bf16[128,2048]{1,0:T(8,128)(2,1)S(1)} %collective-permute-done.3.refs_4_), channel_id=1, source_target_pairs={{0,1},{1,0},{2,3},{3,2},{4,5},{5,4},{6,7},{7,6},{8,9},{9,8},{10,11... | collective-permute-start | bytes 1572872 | tf_op jit(solution)/shard_map/ppermute | solution.py:234
  83.6 8.9 %collective-permute-start.6 = (bf16[128,2048]{1,0:T(8,128)(2,1)S(1)}, bf16[128,2048]{1,0:T(8,128)(2,1)S(1)}, u32[]{:S(2)}, u32[]{:S(2)}) collective-permute-start(bf16[128,2048]{1,0:T(8,128)(2,1)S(1)} %collective-permute-done.5.refs_6_), channel_id=1, source_target_pairs={{0,1},{1,0},{2,3},{3,2},{4,5},{5,4},{6,7},{7,6},{8,9},{9,8},{10,11... | collective-permute-start | bytes 1572872 | tf_op jit(solution)/shard_map/ppermute | solution.py:234
  87.3 11.8 %collective-permute-start.8 = (bf16[128,2048]{1,0:T(8,128)(2,1)S(1)}, bf16[128,2048]{1,0:T(8,128)(2,1)}, u32[]{:S(2)}, u32[]{:S(2)}) collective-permute-start(bf16[128,2048]{1,0:T(8,128)(2,1)S(1)} %collective-permute-done.7.refs_8_), channel_id=1, source_target_pairs={{0,1},{1,0},{2,3},{3,2},{4,5},{5,4},{6,7},{7,6},{8,9},{9,8},{10,11... | collective-permute-start | bytes 1572872 | tf_op jit(solution)/shard_map/ppermute | solution.py:234
  88.3 22.9 %copy-start.9 = (bf16[128,2048]{1,0:T(8,128)(2,1)}, bf16[128,2048]{1,0:T(8,128)(2,1)S(1)}, u32[]{:S(2)}) copy-start(bf16[128,2048]{1,0:T(8,128)(2,1)S(1)} %collective-permute-done.refs_1_) | copy-start | bytes 1572868
  88.4 7.5 %collective-permute-start.13 = (bf16[64,2048]{1,0:T(8,128)(2,1)S(1)}, bf16[64,2048]{1,0:T(8,128)(2,1)S(1)}, u32[]{:S(2)}, u32[]{:S(2)}) collective-permute-start(bf16[64,2048]{1,0:T(8,128)(2,1)S(1)} %slice.8), channel_id=1, source_target_pairs={{0,4},{1,5},{2,0},{3,1},{4,8},{5,9},{6,2},{7,3},{8,12},{9,13},{10,... | collective-permute-start | bytes 786440 | tf_op jit(solution)/shard_map/ppermute | solution.py:224
  89.5 7.6 %collective-permute-start.14 = (bf16[64,2048]{1,0:T(8,128)(2,1)S(1)}, bf16[64,2048]{1,0:T(8,128)(2,1)}, u32[]{:S(2)}, u32[]{:S(2)}) collective-permute-start(bf16[64,2048]{1,0:T(8,128)(2,1)S(1)} %slice.9), channel_id=1, source_target_pairs={{4,0},{5,1},{0,2},{1,3},{8,4},{9,5},{2,6},{3,7},{12,8},{13,9},{6,1... | collective-permute-start | bytes 786440 | tf_op jit(solution)/shard_map/ppermute | solution.py:225
  91.5 8.4 %collective-permute-start.10 = (bf16[128,2048]{1,0:T(8,128)(2,1)}, bf16[128,2048]{1,0:T(8,128)(2,1)}, u32[]{:S(2)}, u32[]{:S(2)}) collective-permute-start(bf16[128,2048]{1,0:T(8,128)(2,1)} %collective-permute-done.9.refs_10_), channel_id=1, source_target_pairs={{0,1},{1,0},{2,3},{3,2},{4,5},{5,4},{6,7},{7,6},{8,9},{9,8},{10,11... | collective-permute-start | bytes 1572872 | tf_op jit(solution)/shard_map/ppermute | solution.py:234
  93.4 6.5 %collective-permute-start.12 = (bf16[128,2048]{1,0:T(8,128)(2,1)}, bf16[128,2048]{1,0:T(8,128)(2,1)}, u32[]{:S(2)}, u32[]{:S(2)}) collective-permute-start(bf16[128,2048]{1,0:T(8,128)(2,1)} %collective-permute-done.11.refs_12_), channel_id=1, source_target_pairs={{0,1},{1,0},{2,3},{3,2},{4,5},{5,4},{6,7},{7,6},{8,9},{9,8},{10,11... | collective-permute-start | bytes 1572872 | tf_op jit(solution)/shard_map/ppermute | solution.py:234
  95.9 3.2 %collective-permute-start.15 = (bf16[64,2048]{1,0:T(8,128)(2,1)S(1)}, bf16[64,2048]{1,0:T(8,128)(2,1)}, u32[]{:S(2)}, u32[]{:S(2)}) collective-permute-start(bf16[64,2048]{1,0:T(8,128)(2,1)S(1)} %collective-permute-done.13.refs_14_), channel_id=1, source_target_pairs={{0,1},{1,0},{2,3},{3,2},{4,5},{5,4},{6,7},{7,6},{8,9},{9,8},{10,11... | collective-permute-start | bytes 786440 | tf_op jit(solution)/shard_map/ppermute | solution.py:234
  97.1 2.7 %collective-permute-start.16 = (bf16[64,2048]{1,0:T(8,128)(2,1)}, bf16[64,2048]{1,0:T(8,128)(2,1)}, u32[]{:S(2)}, u32[]{:S(2)}) collective-permute-start(bf16[64,2048]{1,0:T(8,128)(2,1)} %collective-permute-done.14.refs_15_), channel_id=1, source_target_pairs={{0,1},{1,0},{2,3},{3,2},{4,5},{5,4},{6,7},{7,6},{8,9},{9,8},{10,11... | collective-permute-start | bytes 786440 | tf_op jit(solution)/shard_map/ppermute | solution.py:234
  111.3 41.4 %all-to-all-start = ((bf16[16,128,384]{2,1,0:T(8,128)(2,1)}), bf16[16,128,384]{2,1,0:T(8,128)(2,1)S(1)}, u32[]{:S(2)}, u32[]{:S(2)}) async-start(bf16[16,128,384]{2,1,0:T(8,128)(2,1)} %back_rows.1), calls=%async_computation | async-start | bytes 3145728 | tf_op jit(solution)/shard_map/all_to_all | solution.py:288
  124.8 27.9 %copy-start.1 = (bf16[128,8,384]{2,1,0:T(8,128)(2,1)S(1)}, bf16[128,8,384]{2,1,0:T(8,128)(2,1)}, u32[]{:S(2)}) copy-start(bf16[128,8,384]{2,1,0:T(8,128)(2,1)} %param.7) | copy-start | bytes 2359300
  (17 other events, 37.0 us)

commit v2 on v1

--- a/solution.py
+++ b/solution.py
@@ -9,7 +9,8 @@
 from jax.sharding import PartitionSpec as P
 
 GROUP = 16
-VMEM = 48 * 1024 * 1024
+VMEM = 60 * 1024 * 1024
+SMALL = 12 * 1024 * 1024
 
 
 def padded_on_device(grad_out, hidden, routes, probs, w_down):
@@ -117,7 +118,12 @@
 ):
     span = GROUP * top_count
     inner_width = hidden_ref.shape[1]
-    ones = jnp.ones((8, inner_width), jnp.bfloat16)
+    ones = jnp.ones((top_count, inner_width), jnp.bfloat16)
+    summed = jnp.zeros(prob_ref.shape, jnp.float32)
+    row = lax.broadcasted_iota(jnp.int32, (top_count, span), 0)
+    col = lax.broadcasted_iota(jnp.int32, (top_count, span), 1)
+    slot = lax.broadcasted_iota(jnp.int32, (span, prob_ref.shape[1]), 0)
+    token = lax.broadcasted_iota(jnp.int32, (span, prob_ref.shape[1]), 1)
     across = (((0,), (0,)), ((), ()))
     lanes = (((1,), (1,)), ((), ()))
     for g in range(routes_ref.shape[0]):
@@ -134,7 +140,10 @@
         low = (product - high.astype(jnp.float32)).astype(jnp.bfloat16)
         total = lax.dot_general(ones, high, lanes, preferred_element_type=jnp.float32)
         total += lax.dot_general(ones, low, lanes, preferred_element_type=jnp.float32)
-        prob_ref[g : g + 1, :] = total[0:1, :].astype(jnp.bfloat16)
+        own = jnp.where(col % top_count == row, total, 0.0).astype(jnp.bfloat16)
+        to_token = jnp.where(token == slot // top_count + g * GROUP, 1.0, 0.0)
+        summed += jnp.dot(own, to_token.astype(jnp.bfloat16), preferred_element_type=jnp.float32)
+    prob_ref[...] = summed.astype(jnp.bfloat16)
 
 
 def back_kernel(ids_ref, *refs, places, step):
@@ -219,12 +228,11 @@
         aft = lax.ppermute(aft, "expert", behind)
         own_core += [[(fore, 0, token_count)], [(aft, 0, token_count)]]
         offsets += [-s, s]
-    own_core.append(
-        [
-            (lax.ppermute(fore[:half], "expert", ahead), 0, half),
-            (lax.ppermute(aft[half:], "expert", behind), half, half),
-        ]
-    )
+    late = (
+        lax.ppermute(fore[:half], "expert", ahead),
+        lax.ppermute(aft[half:], "expert", behind),
+    )
+    own_core.append([(late[0], 0, half), (late[1], half, half)])
     offsets.append(chips // 2)
     pieces, places = [], []
     table = np.zeros((peer_count, peer_count), np.int32)
@@ -241,7 +249,7 @@
     ids = lax.dynamic_index_in_dim(
         jnp.asarray(table), lax.axis_index("expert"), 0, keepdims=False
     )
-    return pieces, places, ids
+    return pieces, places, ids, late
 
 
 def dense_on_device(grad_out, hidden, routes, probs, w_down):
@@ -258,19 +266,21 @@
     local_weight = w_down[0]
     sizes = dict(expert_count=peer_count, top_count=top_count)
     params = pltpu.CompilerParams(vmem_limit_bytes=VMEM)
-    anywhere = pl.BlockSpec(memory_space=pl.ANY)
+    small = pltpu.CompilerParams(vmem_limit_bytes=SMALL)
+    anywhere = pl.BlockSpec(memory_space=pltpu.HBM)
     whole = pl.BlockSpec(memory_space=pltpu.VMEM)
 
-    pieces, places, ids = gather_round(grad_out, peer_count)
+    pieces, places, ids, late = gather_round(grad_out, peer_count)
 
     sent_hidden = pl.pallas_call(
         functools.partial(dispatch_kernel, **sizes),
         out_shape=jax.ShapeDtypeStruct((peer_count, token_count, inner_width), jnp.bfloat16),
         in_specs=[whole] * 3,
         out_specs=whole,
-        compiler_params=params,
+        compiler_params=small,
         name="dispatch",
     )(route_rows, prob_rows, hidden_rows)
+    sent_hidden, *_ = lax.optimization_barrier((sent_hidden, *late))
     got_hidden = lax.all_to_all(sent_hidden, "expert", split_axis=0, concat_axis=0, tiled=True)
 
     back = pl.pallas_call(
@@ -306,16 +316,16 @@
         functools.partial(combine_kernel, **sizes),
         out_shape=(
             jax.ShapeDtypeStruct((slot_count, inner_width), jnp.bfloat16),
-            jax.ShapeDtypeStruct((slot_count // span, span), jnp.bfloat16),
+            jax.ShapeDtypeStruct((top_count, token_count), jnp.bfloat16),
         ),
         in_specs=[whole] * 4,
         out_specs=(whole, whole),
-        compiler_params=params,
+        compiler_params=small,
         name="combine",
     )(route_rows, prob_rows, hidden_rows, got_back)
     return (
         grad_hidden.reshape(token_count, top_count, inner_width),
-        grad_probs.reshape(token_count, top_count),
+        grad_probs.T,
         grad_w[None],
     )
 

time: 157 us -> 135 us (0.86)
  local copies, waits for them, and re-layouts: 20.1 us -> 6.76 us
  waiting for transfers between devices: 87 us -> 79.7 us
  Pallas kernels: 20.7 us -> 23.9 us
  starting transfers between devices: 27 us -> 24.1 us
    ppermute x3, waiting for transfers between devices: 64.3 us -> 30.8 us  [gather_round(): fore = lax.ppermute(fore, 'expert', ahead)]
    all_to_all x1, waiting for transfers between devices: 0.01 us -> 18.2 us  [dense_on_device(): lax.all_to_all(sent_hidden, 'expert', split_axis=0, concat_axis=0, tiled=...]
    unnamed x47 -> x30, local copies, waits for them, and re-layouts: 17.2 us -> 5.33 us
    all_to_all x1, waiting for transfers between devices: 19.3 us -> 26.2 us  [dense_on_device(): lax.all_to_all(back, 'expert', split_axis=0, concat_axis=0, tiled=True)]
    ppermute x9, starting transfers between devices: 9.12 us -> 2.83 us  [gather_round(): pieces.append(lax.ppermute(array, 'expert', swap) if j else array)]
    all_to_all x1, starting transfers between devices: 6.71 us -> 10.3 us  [dense_on_device(): lax.all_to_all(sent_hidden, 'expert', split_axis=0, concat_axis=0, tiled=...]
    ppermute x1, waiting for transfers between devices: 2.5 us -> 0.01 us  [gather_round(): lax.ppermute(fore[:half], 'expert', ahead)]
    ppermute x9, waiting for transfers between devices: 0.83 us -> 3.25 us  [gather_round(): pieces.append(lax.ppermute(array, 'expert', swap) if j else array)]
  transfers between devices with their start and end apart: 19 -> 19, of which waited for: 6 -> 12; matrix products, arithmetic and copies ran while one was open for 2% -> 2% of each run, Pallas kernels for 11% -> 16%
where the time goes in v2:
time: 135 us
  waiting for transfers between devices  79.7 us (59%)
  starting transfers between devices  24.1 us (18%)
  Pallas kernels  23.9 us (18%)
  local copies, waits for them, and re-layouts  6.76 us (5%)
    ppermute x3, waiting for transfers between devices, gather_round(): fore = lax.ppermute(fore, 'expert', ahead)  30.8 us
    all_to_all x1, waiting for transfers between devices, dense_on_device(): lax.all_to_all(back, 'expert', split_axis=0, concat_axis=0, tiled=True)  26.2 us
    all_to_all x1, waiting for transfers between devices, dense_on_device(): lax.all_to_all(sent_hidden, 'expert', split_axis=0, concat_axis=0, tiled=...  18.2 us
    all_to_all x1, starting transfers between devices, dense_on_device(): lax.all_to_all(sent_hidden, 'expert', split_axis=0, concat_axis=0, tiled=...  10.3 us
    pallas_call x1, Pallas kernels, dense_on_device(): pl.pallas_call(functools.partial(weight_kernel, places=places, tile=512),...  9.97 us
    pallas_call x1, Pallas kernels, dense_on_device(): pl.pallas_call(functools.partial(back_kernel, places=places, step=4 * tok...  9.39 us
    unnamed x30, local copies, waits for them, and re-layouts  5.33 us
    all_to_all x1, starting transfers between devices, dense_on_device(): lax.all_to_all(back, 'expert', split_axis=0, concat_axis=0, tiled=True)  4.91 us
  transfers between devices with their start and end apart: 19, of which 12 were waited for; matrix products, arithmetic and copies ran while one was open for 2% of the time, Pallas kernels for 16%

profile of v2, /device:TPU:15, one launch (start us, length us, event | category | flops | bytes accessed | tf_op | source)
XLA Modules:
  0.0 135.1 jit_solution(7404562736554293726)
XLA Ops:
  0.9 1.3 collective-permute-start.3
  2.2 11.5 %collective-permute-done.1.refs_2_ = bf16[128,2048]{1,0:T(8,128)(2,1)S(1)} collective-permute-done((bf16[128,2048]{1,0:T(8,128)(2,1)}, bf16[128,2048]{1,0:T(8,128)(2,1)S(1)}, u32[]{:S(2)}, u32[]{:S(2)}) %collective-permute-start.1) | collective-permute-done | bytes 524320 | tf_op jit(solution)/shard_map/ppermute | solution.py:227
  13.9 1.3 collective-permute-start.7
  15.2 10.4 %collective-permute-done.5.refs_6_ = bf16[128,2048]{1,0:T(8,128)(2,1)S(1)} collective-permute-done((bf16[128,2048]{1,0:T(8,128)(2,1)S(1)}, bf16[128,2048]{1,0:T(8,128)(2,1)S(1)}, u32[]{:S(2)}, u32[]{:S(2)}) %collective-permute-start.5) | collective-permute-done | bytes 524320 | tf_op jit(solution)/shard_map/ppermute | solution.py:227
  26.4 1.3 collective-permute-start.11
  27.7 8.9 %collective-permute-done.9.refs_10_ = bf16[128,2048]{1,0:T(8,128)(2,1)S(1)} collective-permute-done((bf16[128,2048]{1,0:T(8,128)(2,1)S(1)}, bf16[128,2048]{1,0:T(8,128)(2,1)S(1)}, u32[]{:S(2)}, u32[]{:S(2)}) %collective-permute-start.9) | collective-permute-done | bytes 524320 | tf_op jit(solution)/shard_map/ppermute | solution.py:227
  37.3 1.3 collective-permute-start.14
  38.7 0.8 copy.11
  39.6 0.8 copy.12
  40.5 1.7 %dispatch.1 = bf16[16,128,384]{2,1,0:T(8,128)(2,1)} custom-call(s32[8,128]{1,0:T(8,128)S(1)} %reshape.18.routes_ref, bf16[8,128]{1,0:T(8,128)(2,1)S(1)} %reshape.19.probs_ref, bf16[1024,384]{1,0:T(8,128)(2,1)S(1)} %bitcast.7), custom_call_target="tpu_custom_call" | custom-call | tf_op jit(solution)/shard_map/dispatch/pallas_call | solution.py:275
  42.2 0.6 collective-permute-done.14.refs_15_
  43.5 10.3 %all-to-all-start.1 = ((bf16[16,128,384]{2,1,0:T(8,128)(2,1)}), bf16[16,128,384]{2,1,0:T(8,128)(2,1)S(1)}, u32[]{:S(2)}, u32[]{:S(2)}) async-start(bf16[16,128,384]{2,1,0:T(8,128)(2,1)} %dispatch.1), calls=%async_computation.1 | async-start | bytes 3145728 | tf_op jit(solution)/shard_map/all_to_all | solution.py:284
  55.3 0.7 collective-permute-done.refs_1_
  57.1 1.1 collective-permute-done.4.refs_5_
  59.1 0.7 collective-permute-done.6.refs_7_
  59.7 0.8 copy-done.11
  60.9 1.2 dynamic-slice_bitcast_fusion.ids_ref
  62.4 9.4 %back_rows.1 = bf16[16,128,384]{2,1,0:T(8,128)(2,1)} custom-call(s32[16]{0:T(128)} %dynamic-slice_bitcast_fusion.ids_ref, bf16[128,2048]{1,0:T(8,128)(2,1)} %refs_0_.3, bf16[128,2048]{1,0:T(8,128)(2,1)} %copy-done.8, bf16[128,2048]{1,0:T(8,128)(2,1)} %copy-done.4, bf16[128,2048]{1,0:T(8,128)(2,1)} %copy-done.9, bf16[128,2048]{1,0:T(8,128)(2,1)} %copy-done.5, ...), custom_call_target="tpu_custom_call" | custom-call | tf_op jit(solution)/shard_map/back_rows/pallas_call | solution.py:286
  71.8 18.2 %all-to-all-done.1.refs_18_ = bf16[16,128,384]{2,1,0:T(8,128)(2,1)S(1)} async-done(((bf16[16,128,384]{2,1,0:T(8,128)(2,1)}), bf16[16,128,384]{2,1,0:T(8,128)(2,1)S(1)}, u32[]{:S(2)}, u32[]{:S(2)}) %all-to-all-start.1) | async-done | bytes 1572896 | tf_op jit(solution)/shard_map/all_to_all | solution.py:284
  90.1 1.1 copy-done.1
  91.2 4.9 %all-to-all-start = ((bf16[16,128,384]{2,1,0:T(8,128)(2,1)}), bf16[16,128,384]{2,1,0:T(8,128)(2,1)S(1)}, u32[]{:S(2)}, u32[]{:S(2)}) async-start(bf16[16,128,384]{2,1,0:T(8,128)(2,1)} %back_rows.1), calls=%async_computation | async-start | bytes 3145728 | tf_op jit(solution)/shard_map/all_to_all | solution.py:298
  96.1 10.0 %grad_w.1 = bf16[384,2048]{1,0:T(8,128)(2,1)} custom-call(s32[16]{0:T(128)} %dynamic-slice_bitcast_fusion.ids_ref, bf16[128,2048]{1,0:T(8,128)(2,1)} %refs_0_.3, bf16[128,2048]{1,0:T(8,128)(2,1)} %copy-done.8, bf16[128,2048]{1,0:T(8,128)(2,1)} %copy-done.4, bf16[128,2048]{1,0:T(8,128)(2,1)} %copy-done.9, bf16[128,2048]{1,0:T(8,128)(2,1)} %copy-done.5, ...), custom_call_target="tpu_custom_call" | custom-call | tf_op jit(solution)/shard_map/grad_w/pallas_call | solution.py:300
  106.1 26.2 %all-to-all-done.back_ref = bf16[16,128,384]{2,1,0:T(8,128)(2,1)S(1)} async-done(((bf16[16,128,384]{2,1,0:T(8,128)(2,1)}), bf16[16,128,384]{2,1,0:T(8,128)(2,1)S(1)}, u32[]{:S(2)}, u32[]{:S(2)}) %all-to-all-start) | async-done | bytes 1572896 | tf_op jit(solution)/shard_map/all_to_all | solution.py:298
  132.3 2.8 %combine.1 = (bf16[1024,384]{1,0:T(8,128)(2,1)}, bf16[8,128]{1,0:T(8,128)(2,1)}) custom-call(s32[8,128]{1,0:T(8,128)S(1)} %reshape.18.routes_ref, bf16[8,128]{1,0:T(8,128)(2,1)S(1)} %reshape.19.probs_ref, bf16[1024,384]{1,0:T(8,128)(2,1)S(1)} %bitcast.8, bf16[16,128,384]{2,1,0:T(8,128)(2,1)S(1)} %all-to-all-done.back_ref), custom_call_target="tpu_custom_call" | custom-call | tf_op jit(solution)/shard_map/combine/pallas_call | solution.py:315
  (53 shorter events, 6.9 us)
Async XLA Ops:
  0.6 39.8 %copy-start = (bf16[128,8,384]{2,1,0:T(8,128)(2,1)S(1)}, bf16[128,8,384]{2,1,0:T(8,128)(2,1)}, u32[]{:S(2)}) copy-start(bf16[128,8,384]{2,1,0:T(8,128)(2,1)} %param.7) | copy-start | bytes 2359300
  0.6 13.1 %collective-permute-start.1 = (bf16[128,2048]{1,0:T(8,128)(2,1)}, bf16[128,2048]{1,0:T(8,128)(2,1)S(1)}, u32[]{:S(2)}, u32[]{:S(2)}) collective-permute-start(bf16[128,2048]{1,0:T(8,128)(2,1)} %refs_0_.3), channel_id=1, source_target_pairs={{0,4},{1,5},{2,0},{3,1},{4,8},{5,9},{6,2},{7,3},{8,12},{9,13},{10,... | collective-permute-start | bytes 1572872 | tf_op jit(solution)/shard_map/ppermute | solution.py:227
  0.9 13.0 %collective-permute-start.3 = (bf16[128,2048]{1,0:T(8,128)(2,1)}, bf16[128,2048]{1,0:T(8,128)(2,1)S(1)}, u32[]{:S(2)}, u32[]{:S(2)}) collective-permute-start(bf16[128,2048]{1,0:T(8,128)(2,1)} %refs_0_.3), channel_id=1, source_target_pairs={{4,0},{5,1},{0,2},{1,3},{8,4},{9,5},{2,6},{3,7},{12,8},{13,9},{6,1... | collective-permute-start | bytes 1572872 | tf_op jit(solution)/shard_map/ppermute | solution.py:228
  13.7 11.9 %collective-permute-start.5 = (bf16[128,2048]{1,0:T(8,128)(2,1)S(1)}, bf16[128,2048]{1,0:T(8,128)(2,1)S(1)}, u32[]{:S(2)}, u32[]{:S(2)}) collective-permute-start(bf16[128,2048]{1,0:T(8,128)(2,1)S(1)} %collective-permute-done.1.refs_2_), channel_id=1, source_target_pairs={{0,4},{1,5},{2,0},{3,1},{4,8},{5,9},{6,2},{7,3},{8,12},{9,13},{10,... | collective-permute-start | bytes 1572872 | tf_op jit(solution)/shard_map/ppermute | solution.py:227
  13.9 11.9 %copy-start.5 = (bf16[128,2048]{1,0:T(8,128)(2,1)}, bf16[128,2048]{1,0:T(8,128)(2,1)S(1)}, u32[]{:S(2)}) copy-start(bf16[128,2048]{1,0:T(8,128)(2,1)S(1)} %collective-permute-done.3.refs_4_) | copy-start | bytes 1572868
  13.9 11.9 %collective-permute-start.7 = (bf16[128,2048]{1,0:T(8,128)(2,1)S(1)}, bf16[128,2048]{1,0:T(8,128)(2,1)S(1)}, u32[]{:S(2)}, u32[]{:S(2)}) collective-permute-start(bf16[128,2048]{1,0:T(8,128)(2,1)S(1)} %collective-permute-done.3.refs_4_), channel_id=1, source_target_pairs={{4,0},{5,1},{0,2},{1,3},{8,4},{9,5},{2,6},{3,7},{12,8},{13,9},{6,1... | collective-permute-start | bytes 1572872 | tf_op jit(solution)/shard_map/ppermute | solution.py:228
  25.6 10.9 %collective-permute-start.9 = (bf16[128,2048]{1,0:T(8,128)(2,1)S(1)}, bf16[128,2048]{1,0:T(8,128)(2,1)S(1)}, u32[]{:S(2)}, u32[]{:S(2)}) collective-permute-start(bf16[128,2048]{1,0:T(8,128)(2,1)S(1)} %collective-permute-done.5.refs_6_), channel_id=1, source_target_pairs={{0,4},{1,5},{2,0},{3,1},{4,8},{5,9},{6,2},{7,3},{8,12},{9,13},{10,... | collective-permute-start | bytes 1572872 | tf_op jit(solution)/shard_map/ppermute | solution.py:227
  26.4 11.0 %copy-start.7 = (bf16[128,2048]{1,0:T(8,128)(2,1)}, bf16[128,2048]{1,0:T(8,128)(2,1)S(1)}, u32[]{:S(2)}) copy-start(bf16[128,2048]{1,0:T(8,128)(2,1)S(1)} %collective-permute-done.7.refs_8_) | copy-start | bytes 1572868
  26.4 10.9 %collective-permute-start.11 = (bf16[128,2048]{1,0:T(8,128)(2,1)S(1)}, bf16[128,2048]{1,0:T(8,128)(2,1)S(1)}, u32[]{:S(2)}, u32[]{:S(2)}) collective-permute-start(bf16[128,2048]{1,0:T(8,128)(2,1)S(1)} %collective-permute-done.7.refs_8_), channel_id=1, source_target_pairs={{4,0},{5,1},{0,2},{1,3},{8,4},{9,5},{2,6},{3,7},{12,8},{13,9},{6,1... | collective-permute-start | bytes 1572872 | tf_op jit(solution)/shard_map/ppermute | solution.py:228
  36.5 19.5 %copy-start.2 = (bf16[128,2048]{1,0:T(8,128)(2,1)}, bf16[128,2048]{1,0:T(8,128)(2,1)S(1)}, u32[]{:S(2)}) copy-start(bf16[128,2048]{1,0:T(8,128)(2,1)S(1)} %collective-permute-done.9.refs_10_) | copy-start | bytes 1572868
  36.5 5.6 %collective-permute-start.13 = (bf16[64,2048]{1,0:T(8,128)(2,1)S(1)}, bf16[64,2048]{1,0:T(8,128)(2,1)S(1)}, u32[]{:S(2)}, u32[]{:S(2)}) collective-permute-start(bf16[64,2048]{1,0:T(8,128)(2,1)S(1)} %slice.8), channel_id=1, source_target_pairs={{0,4},{1,5},{2,0},{3,1},{4,8},{5,9},{6,2},{7,3},{8,12},{9,13},{10,... | collective-permute-start | bytes 786440 | tf_op jit(solution)/shard_map/ppermute | solution.py:232
  37.3 19.4 %copy-start.3 = (bf16[128,2048]{1,0:T(8,128)(2,1)}, bf16[128,2048]{1,0:T(8,128)(2,1)S(1)}, u32[]{:S(2)}) copy-start(bf16[128,2048]{1,0:T(8,128)(2,1)S(1)} %collective-permute-done.11.refs_12_) | copy-start | bytes 1572868
  37.3 5.5 %collective-permute-start.14 = (bf16[64,2048]{1,0:T(8,128)(2,1)S(1)}, bf16[64,2048]{1,0:T(8,128)(2,1)S(1)}, u32[]{:S(2)}, u32[]{:S(2)}) collective-permute-start(bf16[64,2048]{1,0:T(8,128)(2,1)S(1)} %slice.9), channel_id=1, source_target_pairs={{4,0},{5,1},{0,2},{1,3},{8,4},{9,5},{2,6},{3,7},{12,8},{13,9},{6,1... | collective-permute-start | bytes 786440 | tf_op jit(solution)/shard_map/ppermute | solution.py:233
  43.5 46.5 %all-to-all-start.1 = ((bf16[16,128,384]{2,1,0:T(8,128)(2,1)}), bf16[16,128,384]{2,1,0:T(8,128)(2,1)S(1)}, u32[]{:S(2)}, u32[]{:S(2)}) async-start(bf16[16,128,384]{2,1,0:T(8,128)(2,1)} %dispatch.1), calls=%async_computation.1 | async-start | bytes 3145728 | tf_op jit(solution)/shard_map/all_to_all | solution.py:284
  53.9 2.1 %collective-permute-start = (bf16[128,2048]{1,0:T(8,128)(2,1)}, bf16[128,2048]{1,0:T(8,128)(2,1)S(1)}, u32[]{:S(2)}, u32[]{:S(2)}) collective-permute-start(bf16[128,2048]{1,0:T(8,128)(2,1)} %refs_0_.3), channel_id=1, source_target_pairs={{0,1},{1,0},{2,3},{3,2},{4,5},{5,4},{6,7},{7,6},{8,9},{9,8},{10,11... | collective-permute-start | bytes 1572872 | tf_op jit(solution)/shard_map/ppermute | solution.py:242
  54.2 2.5 %collective-permute-start.2 = (bf16[128,2048]{1,0:T(8,128)(2,1)}, bf16[128,2048]{1,0:T(8,128)(2,1)S(1)}, u32[]{:S(2)}, u32[]{:S(2)}) collective-permute-start(bf16[128,2048]{1,0:T(8,128)(2,1)} %copy-done.4), channel_id=1, source_target_pairs={{0,1},{1,0},{2,3},{3,2},{4,5},{5,4},{6,7},{7,6},{8,9},{9,8},{10,11... | collective-permute-start | bytes 1572872 | tf_op jit(solution)/shard_map/ppermute | solution.py:242
  54.4 3.9 %collective-permute-start.4 = (bf16[128,2048]{1,0:T(8,128)(2,1)}, bf16[128,2048]{1,0:T(8,128)(2,1)S(1)}, u32[]{:S(2)}, u32[]{:S(2)}) collective-permute-start(bf16[128,2048]{1,0:T(8,128)(2,1)} %copy-done.5), channel_id=1, source_target_pairs={{0,1},{1,0},{2,3},{3,2},{4,5},{5,4},{6,7},{7,6},{8,9},{9,8},{10,11... | collective-permute-start | bytes 1572872 | tf_op jit(solution)/shard_map/ppermute | solution.py:242
  54.7 5.0 %collective-permute-start.6 = (bf16[128,2048]{1,0:T(8,128)(2,1)}, bf16[128,2048]{1,0:T(8,128)(2,1)S(1)}, u32[]{:S(2)}, u32[]{:S(2)}) collective-permute-start(bf16[128,2048]{1,0:T(8,128)(2,1)} %copy-done.6), channel_id=1, source_target_pairs={{0,1},{1,0},{2,3},{3,2},{4,5},{5,4},{6,7},{7,6},{8,9},{9,8},{10,11... | collective-permute-start | bytes 1572872 | tf_op jit(solution)/shard_map/ppermute | solution.py:242
  54.9 7.2 %collective-permute-start.8 = (bf16[128,2048]{1,0:T(8,128)(2,1)}, bf16[128,2048]{1,0:T(8,128)(2,1)}, u32[]{:S(2)}, u32[]{:S(2)}) collective-permute-start(bf16[128,2048]{1,0:T(8,128)(2,1)} %copy-done.7), channel_id=1, source_target_pairs={{0,1},{1,0},{2,3},{3,2},{4,5},{5,4},{6,7},{7,6},{8,9},{9,8},{10,11... | collective-permute-start | bytes 1572872 | tf_op jit(solution)/shard_map/ppermute | solution.py:242
  56.0 6.4 %collective-permute-start.10 = (bf16[128,2048]{1,0:T(8,128)(2,1)S(1)}, bf16[128,2048]{1,0:T(8,128)(2,1)}, u32[]{:S(2)}, u32[]{:S(2)}) collective-permute-start(bf16[128,2048]{1,0:T(8,128)(2,1)S(1)} %collective-permute-done.9.refs_10_), channel_id=1, source_target_pairs={{0,1},{1,0},{2,3},{3,2},{4,5},{5,4},{6,7},{7,6},{8,9},{9,8},{10,11... | collective-permute-start | bytes 1572872 | tf_op jit(solution)/shard_map/ppermute | solution.py:242
  56.7 5.7 %collective-permute-start.12 = (bf16[128,2048]{1,0:T(8,128)(2,1)S(1)}, bf16[128,2048]{1,0:T(8,128)(2,1)}, u32[]{:S(2)}, u32[]{:S(2)}) collective-permute-start(bf16[128,2048]{1,0:T(8,128)(2,1)S(1)} %collective-permute-done.11.refs_12_), channel_id=1, source_target_pairs={{0,1},{1,0},{2,3},{3,2},{4,5},{5,4},{6,7},{7,6},{8,9},{9,8},{10,11... | collective-permute-start | bytes 1572872 | tf_op jit(solution)/shard_map/ppermute | solution.py:242
  58.2 3.9 %collective-permute-start.15 = (bf16[64,2048]{1,0:T(8,128)(2,1)}, bf16[64,2048]{1,0:T(8,128)(2,1)}, u32[]{:S(2)}, u32[]{:S(2)}) collective-permute-start(bf16[64,2048]{1,0:T(8,128)(2,1)} %copy-done.12), channel_id=1, source_target_pairs={{0,1},{1,0},{2,3},{3,2},{4,5},{5,4},{6,7},{7,6},{8,9},{9,8},{10,11... | collective-permute-start | bytes 786440 | tf_op jit(solution)/shard_map/ppermute | solution.py:242
  60.5 1.9 %collective-permute-start.16 = (bf16[64,2048]{1,0:T(8,128)(2,1)}, bf16[64,2048]{1,0:T(8,128)(2,1)}, u32[]{:S(2)}, u32[]{:S(2)}) collective-permute-start(bf16[64,2048]{1,0:T(8,128)(2,1)} %copy-done.13), channel_id=1, source_target_pairs={{0,1},{1,0},{2,3},{3,2},{4,5},{5,4},{6,7},{7,6},{8,9},{9,8},{10,11... | collective-permute-start | bytes 786440 | tf_op jit(solution)/shard_map/ppermute | solution.py:242
  91.2 41.1 %all-to-all-start = ((bf16[16,128,384]{2,1,0:T(8,128)(2,1)}), bf16[16,128,384]{2,1,0:T(8,128)(2,1)S(1)}, u32[]{:S(2)}, u32[]{:S(2)}) async-start(bf16[16,128,384]{2,1,0:T(8,128)(2,1)} %back_rows.1), calls=%async_computation | async-start | bytes 3145728 | tf_op jit(solution)/shard_map/all_to_all | solution.py:298
  (9 other events, 9.1 us)

commit v3 on v2

--- a/solution.py
+++ b/solution.py
@@ -8,7 +8,9 @@
 from jax.experimental.pallas import tpu as pltpu
 from jax.sharding import PartitionSpec as P
 
+TILE = 512
 GROUP = 16
+SPLIT = 1
 VMEM = 60 * 1024 * 1024
 SMALL = 12 * 1024 * 1024
 
@@ -113,9 +115,8 @@
         out_ref[:, g * GROUP : (g + 1) * GROUP, :] = rows.reshape(expert_count, GROUP, inner_width)
 
 
-def combine_kernel(
-    routes_ref, probs_ref, hidden_ref, back_ref, hid_ref, prob_ref, *, expert_count, top_count
-):
+def combine_kernel(routes_ref, probs_ref, hidden_ref, *refs, top_count):
+    back_refs, (hid_ref, prob_ref) = refs[:-2], refs[-2:]
     span = GROUP * top_count
     inner_width = hidden_ref.shape[1]
     ones = jnp.ones((top_count, inner_width), jnp.bfloat16)
@@ -127,10 +128,12 @@
     across = (((0,), (0,)), ((), ()))
     lanes = (((1,), (1,)), ((), ()))
     for g in range(routes_ref.shape[0]):
-        chosen = chosen_slots(routes_ref[g : g + 1, :], expert_count, top_count)
+        chosen = chosen_slots(routes_ref[g : g + 1, :], len(back_refs), top_count)
         pick = jnp.where(chosen, 1.0, 0.0).astype(jnp.bfloat16)
         scaled = jnp.where(chosen, probs_ref[g : g + 1, :].astype(jnp.float32), 0.0)
-        block = back_ref[:, g * GROUP : (g + 1) * GROUP, :].reshape(expert_count * GROUP, inner_width)
+        block = jnp.concatenate(
+            [ref[g * GROUP : (g + 1) * GROUP, :] for ref in back_refs], axis=0
+        )
         mine = lax.dot_general(pick, block, across, preferred_element_type=jnp.float32)
         hid_ref[g * span : (g + 1) * span, :] = lax.dot_general(
             scaled.astype(jnp.bfloat16), block, across, preferred_element_type=jnp.float32
@@ -146,15 +149,15 @@
     prob_ref[...] = summed.astype(jnp.bfloat16)
 
 
-def back_kernel(ids_ref, *refs, places, step):
-    pieces, (w_ref, out_ref, held, sems) = refs[: len(places)], refs[len(places) :]
+def back_kernel(order_ref, *refs, places, step, block):
+    pieces, w_ref = refs[: len(places)], refs[len(places)]
+    out_refs, (held, rows_held, sems) = refs[len(places) + 1 : -3], refs[-3:]
     copies = []
     for i, (first, rows) in enumerate(places):
         copies.append(
             pltpu.make_async_copy(pieces[i], held.at[pl.ds(first, rows)], sems.at[i])
         )
         copies[i].start()
-    block = out_ref.shape[1]
     waited = 0
     for first in range(0, held.shape[0], step):
         while waited < len(places) and places[waited][0] < first + step:
@@ -167,15 +170,16 @@
             preferred_element_type=jnp.float32,
         ).astype(jnp.bfloat16)
         for j in range(step // block):
-            out_ref[ids_ref[first // block + j]] = rows[j * block : (j + 1) * block, :]
-
-
-def weight_kernel(ids_ref, *refs, places, tile):
-    pieces, (hidden_ref, out_ref, held, rows_held, sems, row_sems) = (
-        refs[: len(places)],
-        refs[len(places) :],
-    )
+            rows_held[first // block + j] = rows[j * block : (j + 1) * block, :]
+    for k, out_ref in enumerate(out_refs):
+        out_ref[...] = rows_held[order_ref[k]]
+
+
+def weight_kernel(ids_ref, *refs, places, first_col):
+    hidden_ref, out_ref, held, rows_held, sems, row_sems = refs[-6:]
+    pieces = refs[: len(places)]
     block = hidden_ref.shape[1]
+    cols = pl.ds(first_col, out_ref.shape[1])
     copies = []
     for j in range(hidden_ref.shape[0]):
         copies.append(
@@ -185,19 +189,20 @@
         )
     for i, (first, rows) in enumerate(places):
         copies.append(
-            pltpu.make_async_copy(pieces[i], held.at[pl.ds(first, rows)], sems.at[i])
+            pltpu.make_async_copy(pieces[i].at[:, cols], held.at[pl.ds(first, rows)], sems.at[i])
         )
     for copy in copies:
         copy.start()
     for copy in copies:
         copy.wait()
+    tile = min(TILE, out_ref.shape[1])
 
     @pl.loop(0, out_ref.shape[1] // tile)
     def _(n):
-        cols = pl.ds(pl.multiple_of(n * tile, tile), tile)
-        out_ref[:, cols] = lax.dot_general(
+        part = pl.ds(pl.multiple_of(n * tile, tile), tile)
+        out_ref[:, part] = lax.dot_general(
             rows_held[...],
-            held[:, cols],
+            held[:, part],
             (((0,), (0,)), ((), ())),
             preferred_element_type=jnp.float32,
         ).astype(jnp.bfloat16)
@@ -220,17 +225,25 @@
     ]
     behind = [(b, a) for a, b in ahead]
     swap = [(i, i ^ 1) for i in range(peer_count)]
-    offsets, own_core = [0], []
-    own_core.append([(grad_out, 0, token_count)])
-    fore = aft = grad_out
+    low, high = grad_out[:half], grad_out[half:]
+    offsets, own_core = [0], [[(low, 0, half), (high, half, half)]]
+    low_fore = low_aft = low
+    high_fore = high_aft = high
     for s in range(1, chips // 2):
-        fore = lax.ppermute(fore, "expert", ahead)
-        aft = lax.ppermute(aft, "expert", behind)
-        own_core += [[(fore, 0, token_count)], [(aft, 0, token_count)]]
+        low_fore = lax.ppermute(low_fore, "expert", ahead)
+        high_aft = lax.ppermute(high_aft, "expert", behind)
+        high_fore = lax.ppermute(high_fore, "expert", ahead)
+        low_aft = lax.ppermute(low_aft, "expert", behind)
+        own_core += [
+            [(low_fore, 0, half), (high_fore, half, half)],
+            [(low_aft, 0, half), (high_aft, half, half)],
+        ]
         offsets += [-s, s]
     late = (
-        lax.ppermute(fore[:half], "expert", ahead),
-        lax.ppermute(aft[half:], "expert", behind),
+        lax.ppermute(low_fore, "expert", ahead),
+        lax.ppermute(high_aft, "expert", behind),
+        high_fore,
+        low_aft,
     )
     own_core.append([(late[0], 0, half), (late[1], half, half)])
     offsets.append(chips // 2)
@@ -246,10 +259,12 @@
             source = ring[(place[chip] + offsets[i]) % chips]
             table[peer, 2 * i] = 2 * source + core
             table[peer, 2 * i + 1] = 2 * source + 1 - core
-    ids = lax.dynamic_index_in_dim(
-        jnp.asarray(table), lax.axis_index("expert"), 0, keepdims=False
-    )
-    return pieces, places, ids, late
+    return pieces, places, table, late
+
+
+def exchange(blocks, some):
+    peers = range(len(blocks))
+    return {k: lax.ppermute(blocks[k], "expert", [(i, i ^ k) for i in peers]) for k in some}
 
 
 def dense_on_device(grad_out, hidden, routes, probs, w_down):
@@ -260,69 +275,99 @@
     slot_count = token_count * top_count
     row_count = peer_count * token_count
     span = GROUP * top_count
+    me = lax.axis_index("expert")
     route_rows = routes.reshape(slot_count // span, span)
     prob_rows = probs.reshape(slot_count // span, span)
     hidden_rows = hidden.reshape(slot_count, inner_width)
     local_weight = w_down[0]
-    sizes = dict(expert_count=peer_count, top_count=top_count)
     params = pltpu.CompilerParams(vmem_limit_bytes=VMEM)
     small = pltpu.CompilerParams(vmem_limit_bytes=SMALL)
-    anywhere = pl.BlockSpec(memory_space=pltpu.HBM)
+    scalars = pl.BlockSpec(memory_space=pltpu.SMEM)
     whole = pl.BlockSpec(memory_space=pltpu.VMEM)
-
-    pieces, places, ids, late = gather_round(grad_out, peer_count)
-
-    sent_hidden = pl.pallas_call(
-        functools.partial(dispatch_kernel, **sizes),
+    far = pl.BlockSpec(memory_space=pltpu.HBM)
+    block = jax.ShapeDtypeStruct((token_count, inner_width), jnp.bfloat16)
+
+    pieces, places, table, late = gather_round(grad_out, peer_count)
+    ids = lax.dynamic_index_in_dim(jnp.asarray(table), me, 0, keepdims=False)
+    order = np.stack([np.argsort(table[peer] ^ peer) for peer in range(peer_count)])
+    order = lax.dynamic_index_in_dim(
+        jnp.asarray(order.astype(np.int32)), me, 0, keepdims=False
+    )
+
+    sent = pl.pallas_call(
+        functools.partial(dispatch_kernel, expert_count=peer_count, top_count=top_count),
         out_shape=jax.ShapeDtypeStruct((peer_count, token_count, inner_width), jnp.bfloat16),
         in_specs=[whole] * 3,
         out_specs=whole,
         compiler_params=small,
         name="dispatch",
     )(route_rows, prob_rows, hidden_rows)
-    sent_hidden, *_ = lax.optimization_barrier((sent_hidden, *late))
-    got_hidden = lax.all_to_all(sent_hidden, "expert", split_axis=0, concat_axis=0, tiled=True)
+    sent, _ = lax.optimization_barrier((sent, late))
+    got_hidden = lax.all_to_all(sent, "expert", split_axis=0, concat_axis=0, tiled=True)
 
     back = pl.pallas_call(
-        functools.partial(back_kernel, places=places, step=4 * token_count),
-        out_shape=jax.ShapeDtypeStruct((peer_count, token_count, inner_width), jnp.bfloat16),
-        in_specs=[pl.BlockSpec(memory_space=pltpu.SMEM)] + [anywhere] * len(pieces) + [whole],
-        out_specs=whole,
+        functools.partial(back_kernel, places=places, step=4 * token_count, block=token_count),
+        out_shape=[block] * peer_count,
+        in_specs=[scalars] + [far] * len(pieces) + [whole],
+        out_specs=[whole] * peer_count,
         scratch_shapes=[
             pltpu.VMEM((row_count, model_width), jnp.bfloat16),
+            pltpu.VMEM((peer_count, token_count, inner_width), jnp.bfloat16),
             pltpu.SemaphoreType.DMA((len(pieces),)),
         ],
         compiler_params=params,
+        cost_estimate=pl.CostEstimate(
+            flops=2 * row_count * inner_width * model_width,
+            bytes_accessed=2 * (row_count + inner_width) * model_width,
+            transcendentals=0,
+        ),
         name="back_rows",
-    )(ids, *pieces, local_weight)
-    got_back = lax.all_to_all(back, "expert", split_axis=0, concat_axis=0, tiled=True)
-
-    grad_w = pl.pallas_call(
-        functools.partial(weight_kernel, places=places, tile=512),
-        out_shape=jax.ShapeDtypeStruct((inner_width, model_width), jnp.bfloat16),
-        in_specs=[pl.BlockSpec(memory_space=pltpu.SMEM)] + [anywhere] * (len(pieces) + 1),
-        out_specs=whole,
-        scratch_shapes=[
-            pltpu.VMEM((row_count, model_width), jnp.bfloat16),
-            pltpu.VMEM((row_count, inner_width), jnp.bfloat16),
-            pltpu.SemaphoreType.DMA((len(pieces),)),
-            pltpu.SemaphoreType.DMA((peer_count,)),
-        ],
-        compiler_params=params,
-        name="grad_w",
-    )(ids, *pieces, got_hidden)
-
+    )(order, *pieces, local_weight)
+    held_back = range(peer_count - 3, peer_count)
+    got_back = {0: back[0]} | exchange(back, [k for k in range(1, peer_count) if k not in held_back])
+
+    near = {k: got_back[k] for k in range(1, peer_count // 2)}
+    got_hidden, near = lax.optimization_barrier((got_hidden, near))
+    got_back |= near
+    width = model_width // SPLIT
+    grad_w = [
+        pl.pallas_call(
+            functools.partial(weight_kernel, places=places, first_col=n * width),
+            out_shape=jax.ShapeDtypeStruct((inner_width, width), jnp.bfloat16),
+            in_specs=[scalars] + [far] * len(pieces) + [pl.BlockSpec(memory_space=pl.ANY)],
+            out_specs=whole,
+            scratch_shapes=[
+                pltpu.VMEM((row_count, width), jnp.bfloat16),
+                pltpu.VMEM((row_count, inner_width), jnp.bfloat16),
+                pltpu.SemaphoreType.DMA((len(pieces),)),
+                pltpu.SemaphoreType.DMA((peer_count,)),
+            ],
+            compiler_params=params,
+            cost_estimate=pl.CostEstimate(
+                flops=2 * row_count * inner_width * width,
+                bytes_accessed=2 * (row_count * (width + inner_width) + inner_width * width),
+                transcendentals=0,
+            ),
+            name="grad_w",
+        )(ids, *pieces, got_hidden)
+        for n in range(SPLIT)
+    ]
+    grad_w = jnp.concatenate(grad_w, axis=1) if SPLIT > 1 else grad_w[0]
+
+    back, grad_w = lax.optimization_barrier((back, grad_w))
+    got_back |= exchange(back, held_back)
+    got_back = [got_back[k] for k in range(peer_count)]
     grad_hidden, grad_probs = pl.pallas_call(
-        functools.partial(combine_kernel, **sizes),
+        functools.partial(combine_kernel, top_count=top_count),
         out_shape=(
             jax.ShapeDtypeStruct((slot_count, inner_width), jnp.bfloat16),
             jax.ShapeDtypeStruct((top_count, token_count), jnp.bfloat16),
         ),
-        in_specs=[whole] * 4,
+        in_specs=[whole] * (3 + peer_count),
         out_specs=(whole, whole),
         compiler_params=small,
         name="combine",
-    )(route_rows, prob_rows, hidden_rows, got_back)
+    )((routes ^ me).reshape(slot_count // span, span), prob_rows, hidden_rows, *got_back)
     return (
         grad_hidden.reshape(token_count, top_count, inner_width),
         grad_probs.T,
@@ -338,6 +383,7 @@
         2 * top_count >= peer_count
         and lax.axis_size("dp") == 1
         and peer_count % 4 == 0
+        and peer_count & (peer_count - 1) == 0
         and token_count % (2 * GROUP) == 0
         and (GROUP * top_count) % 128 == 0
     )

time: 135 us -> 125 us (0.926)
  waiting for transfers between devices: 79.7 us -> 54.1 us
  starting transfers between devices: 24.1 us -> 39.5 us
  local copies, waits for them, and re-layouts: 6.76 us -> 5 us
    all_to_all x2 -> x1, waiting for transfers between devices: 44.4 us -> 8.31 us  [dense_on_device(): lax.all_to_all(sent, 'expert', split_axis=0, concat_axis=0, tiled=True)]
    ppermute x8 -> x29, starting transfers between devices: 6.02 us -> 27.5 us  [the longest x15 17.2 us: exchange(): lax.ppermute(blocks[k], 'expert', [(i, i ^ k) for i in peers])]
    ppermute x8 -> x29, waiting for transfers between devices: 32 us -> 44.9 us  [the longest x15 16.7 us: exchange(): lax.ppermute(blocks[k], 'expert', [(i, i ^ k) for i in peers])]
    all_to_all x2 -> x1, starting transfers between devices: 15.3 us -> 6.73 us  [dense_on_device(): lax.all_to_all(sent, 'expert', split_axis=0, concat_axis=0, tiled=True)]
    unnamed x30 -> x60, local copies, waits for them, and re-layouts: 5.33 us -> 2.21 us
    ppermute x9 -> x16, starting transfers between devices: 2.83 us -> 5.27 us  [gather_round(): pieces.append(lax.ppermute(array, 'expert', swap) if j else array)]
    ppermute x9 -> x16, waiting for transfers between devices: 3.25 us -> 0.92 us  [gather_round(): pieces.append(lax.ppermute(array, 'expert', swap) if j else array)]
  transfers between devices with their start and end apart: 19 -> 46, of which waited for: 12 -> 19; matrix products, arithmetic and copies ran while one was open for 2% -> 3% of each run, Pallas kernels for 16% -> 17%
where the time goes in v3:
time: 125 us; the launch traced here: 124 us
  waiting for transfers between devices  54.1 us (43%)
  starting transfers between devices  39.5 us (32%)
  Pallas kernels  24.4 us (20%)
  local copies, waits for them, and re-layouts  5 us (4%)
    ppermute x15, starting transfers between devices, exchange(): lax.ppermute(blocks[k], 'expert', [(i, i ^ k) for i in peers])  17.2 us
    ppermute x15, waiting for transfers between devices, exchange(): lax.ppermute(blocks[k], 'expert', [(i, i ^ k) for i in peers])  16.7 us
    ppermute x3, waiting for transfers between devices, gather_round(): high_fore = lax.ppermute(high_fore, 'expert', ahead)  12.1 us
    ppermute x3, waiting for transfers between devices, gather_round(): high_aft = lax.ppermute(high_aft, 'expert', behind)  10.5 us
    pallas_call x1, Pallas kernels, dense_on_device(): pl.pallas_call(functools.partial(weight_kernel, places=places, first_col=...  10.4 us
    pallas_call x1, Pallas kernels, dense_on_device(): pl.pallas_call(functools.partial(back_kernel, places=places, step=4 * tok...  9.49 us
    all_to_all x1, waiting for transfers between devices, dense_on_device(): lax.all_to_all(sent, 'expert', split_axis=0, concat_axis=0, tiled=True)  8.31 us
    all_to_all x1, starting transfers between devices, dense_on_device(): lax.all_to_all(sent, 'expert', split_axis=0, concat_axis=0, tiled=True)  6.73 us
  transfers between devices with their start and end apart: 46, of which 19 were waited for; matrix products, arithmetic and copies ran while one was open for 3% of the time, Pallas kernels for 17%

profile of v3, /device:TPU:15, one launch (start us, length us, event | category | flops | bytes accessed | tf_op | source)
XLA Modules:
  0.0 123.9 jit_solution(9188219761607789939)
XLA Ops:
  1.8 1.3 %collective-permute-start.7 = (bf16[64,2048]{1,0:T(8,128)(2,1)S(1)}, bf16[64,2048]{1,0:T(8,128)(2,1)S(1)}, u32[]{:S(2)}, u32[]{:S(2)}) collective-permute-start(bf16[64,2048]{1,0:T(8,128)(2,1)S(1)} %get-tuple-element.65.refs_1_), channel_id=1, source_target_pairs={{4,0},{5,1},{0,2},{1,3},{8,4},{9,5},{2,6},{3,7},{12,8},{13,9},{6,1... | collective-permute-start | bytes 786440 | tf_op jit(solution)/shard_map/ppermute | solution.py:234
  4.8 4.2 %collective-permute-done.7.refs_9_ = bf16[64,2048]{1,0:T(8,128)(2,1)S(1)} collective-permute-done((bf16[64,2048]{1,0:T(8,128)(2,1)S(1)}, bf16[64,2048]{1,0:T(8,128)(2,1)S(1)}, u32[]{:S(2)}, u32[]{:S(2)}) %collective-permute-start.7) | collective-permute-done | bytes 262176 | tf_op jit(solution)/shard_map/ppermute | solution.py:234
  10.5 5.1 %collective-permute-done.3.refs_5_ = bf16[64,2048]{1,0:T(8,128)(2,1)S(1)} collective-permute-done((bf16[64,2048]{1,0:T(8,128)(2,1)S(1)}, bf16[64,2048]{1,0:T(8,128)(2,1)S(1)}, u32[]{:S(2)}, u32[]{:S(2)}) %collective-permute-start.3) | collective-permute-done | bytes 262176 | tf_op jit(solution)/shard_map/ppermute | solution.py:235
  15.8 1.3 %collective-permute-start.14 = (bf16[64,2048]{1,0:T(8,128)(2,1)S(1)}, bf16[64,2048]{1,0:T(8,128)(2,1)}, u32[]{:S(2)}, u32[]{:S(2)}) collective-permute-start(bf16[64,2048]{1,0:T(8,128)(2,1)S(1)} %collective-permute-done.6.refs_8_), channel_id=1, source_target_pairs={{4,0},{5,1},{0,2},{1,3},{8,4},{9,5},{2,6},{3,7},{12,8},{13,9},{6,1... | collective-permute-start | bytes 786440 | tf_op jit(solution)/shard_map/ppermute | solution.py:236
  17.1 3.2 %collective-permute-done.15.refs_17_ = bf16[64,2048]{1,0:T(8,128)(2,1)S(1)} collective-permute-done((bf16[64,2048]{1,0:T(8,128)(2,1)S(1)}, bf16[64,2048]{1,0:T(8,128)(2,1)S(1)}, u32[]{:S(2)}, u32[]{:S(2)}) %collective-permute-start.15) | collective-permute-done | bytes 262176 | tf_op jit(solution)/shard_map/ppermute | solution.py:234
  21.7 5.2 %collective-permute-done.11.refs_13_ = bf16[64,2048]{1,0:T(8,128)(2,1)S(1)} collective-permute-done((bf16[64,2048]{1,0:T(8,128)(2,1)S(1)}, bf16[64,2048]{1,0:T(8,128)(2,1)S(1)}, u32[]{:S(2)}, u32[]{:S(2)}) %collective-permute-start.11) | collective-permute-done | bytes 262176 | tf_op jit(solution)/shard_map/ppermute | solution.py:235
  27.1 1.3 %collective-permute-start.22 = (bf16[64,2048]{1,0:T(8,128)(2,1)}, bf16[64,2048]{1,0:T(8,128)(2,1)}, u32[]{:S(2)}, u32[]{:S(2)}) collective-permute-start(bf16[64,2048]{1,0:T(8,128)(2,1)} %collective-permute-done.14.refs_16_), channel_id=1, source_target_pairs={{4,0},{5,1},{0,2},{1,3},{8,4},{9,5},{2,6},{3,7},{12,8},{13,9},{6,1... | collective-permute-start | bytes 786440 | tf_op jit(solution)/shard_map/ppermute | solution.py:236
  28.4 3.1 %collective-permute-done.23.refs_25_ = bf16[64,2048]{1,0:T(8,128)(2,1)} collective-permute-done((bf16[64,2048]{1,0:T(8,128)(2,1)S(1)}, bf16[64,2048]{1,0:T(8,128)(2,1)}, u32[]{:S(2)}, u32[]{:S(2)}) %collective-permute-start.23) | collective-permute-done | bytes 262176 | tf_op jit(solution)/shard_map/ppermute | solution.py:234
  34.8 1.7 %dispatch.1 = bf16[16,128,384]{2,1,0:T(8,128)(2,1)} custom-call(s32[8,128]{1,0:T(8,128)S(1)} %reshape.24.routes_ref, bf16[8,128]{1,0:T(8,128)(2,1)S(1)} %reshape.22.probs_ref, bf16[1024,384]{1,0:T(8,128)(2,1)S(1)} %bitcast.9), custom_call_target="tpu_custom_call" | custom-call | tf_op jit(solution)/shard_map/dispatch/pallas_call | solution.py:297
  36.5 1.7 %collective-permute-done.19.refs_21_ = bf16[64,2048]{1,0:T(8,128)(2,1)} collective-permute-done((bf16[64,2048]{1,0:T(8,128)(2,1)S(1)}, bf16[64,2048]{1,0:T(8,128)(2,1)}, u32[]{:S(2)}, u32[]{:S(2)}) %collective-permute-start.19) | collective-permute-done | bytes 262176 | tf_op jit(solution)/shard_map/ppermute | solution.py:235
  38.2 4.3 %collective-permute-done.27.refs_29_ = bf16[64,2048]{1,0:T(8,128)(2,1)} collective-permute-done((bf16[64,2048]{1,0:T(8,128)(2,1)}, bf16[64,2048]{1,0:T(8,128)(2,1)}, u32[]{:S(2)}, u32[]{:S(2)}) %collective-permute-start.27) | collective-permute-done | bytes 262176 | tf_op jit(solution)/shard_map/ppermute | solution.py:244
  43.8 6.7 %all-to-all-start = ((bf16[16,128,384]{2,1,0:T(8,128)(2,1)}), bf16[16,128,384]{2,1,0:T(8,128)(2,1)}, u32[]{:S(2)}, u32[]{:S(2)}) async-start(bf16[16,128,384]{2,1,0:T(8,128)(2,1)} %dispatch.1), calls=%async_computation | async-start | bytes 3145728 | tf_op jit(solution)/shard_map/all_to_all | solution.py:306
  58.7 9.5 %back_rows.1 = (bf16[128,384]{1,0:T(8,128)(2,1)}, bf16[128,384]{1,0:T(8,128)(2,1)}, bf16[128,384]{1,0:T(8,128)(2,1)}, bf16[128,384]{1,0:T(8,128)(2,1)}, bf16[128...) custom-call(s32[16]{0:T(128)} %get-tuple-element.68.order_ref, ...), custom_call_target="tpu_custom_call" | custom-call | flops 3221225472 | bytes 9961472 | tf_op jit(solution)/shard_map/back_rows/pallas_call | solution.py:308
  68.7 1.7 %collective-permute-start.32 = (bf16[128,384]{1,0:T(8,128)(2,1)}, bf16[128,384]{1,0:T(8,128)(2,1)S(1)}, u32[]{:S(2)}, u32[]{:S(2)}) collective-permute-start(bf16[128,384]{1,0:T(8,128)(2,1)} %get-tuple-element.38), channel_id=1, source_target_pairs={{0,3},{1,2},{2,1},{3,0},{4,7},{5,6},{6,5},{7,4},{8,11},{9,10},{10,... | collective-permute-start | bytes 294920 | tf_op jit(solution)/shard_map/ppermute | solution.py:267
  72.7 3.1 %collective-permute-start.36 = (bf16[128,384]{1,0:T(8,128)(2,1)}, bf16[128,384]{1,0:T(8,128)(2,1)S(1)}, u32[]{:S(2)}, u32[]{:S(2)}) collective-permute-start(bf16[128,384]{1,0:T(8,128)(2,1)} %get-tuple-element.42), channel_id=1, source_target_pairs={{0,7},{1,6},{2,5},{3,4},{4,3},{5,2},{6,1},{7,0},{8,15},{9,14},{10,... | collective-permute-start | bytes 294920 | tf_op jit(solution)/shard_map/ppermute | solution.py:267
  75.9 3.9 %collective-permute-done.32.refs_3_ = bf16[128,384]{1,0:T(8,128)(2,1)S(1)} collective-permute-done((bf16[128,384]{1,0:T(8,128)(2,1)}, bf16[128,384]{1,0:T(8,128)(2,1)S(1)}, u32[]{:S(2)}, u32[]{:S(2)}) %collective-permute-start.32) | collective-permute-done | bytes 98336 | tf_op jit(solution)/shard_map/ppermute | solution.py:267
  79.8 2.2 %collective-permute-start.38 = (bf16[128,384]{1,0:T(8,128)(2,1)}, bf16[128,384]{1,0:T(8,128)(2,1)S(1)}, u32[]{:S(2)}, u32[]{:S(2)}) collective-permute-start(bf16[128,384]{1,0:T(8,128)(2,1)} %get-tuple-element.51), channel_id=1, source_target_pairs={{0,9},{1,8},{2,11},{3,10},{4,13},{5,12},{6,15},{7,14},{8,1},{9,0},... | collective-permute-start | bytes 294920 | tf_op jit(solution)/shard_map/ppermute | solution.py:267
  82.4 6.0 %collective-permute-start.39 = (bf16[128,384]{1,0:T(8,128)(2,1)}, bf16[128,384]{1,0:T(8,128)(2,1)S(1)}, u32[]{:S(2)}, u32[]{:S(2)}) collective-permute-start(bf16[128,384]{1,0:T(8,128)(2,1)} %get-tuple-element.52), channel_id=1, source_target_pairs={{0,10},{1,11},{2,8},{3,9},{4,14},{5,15},{6,12},{7,13},{8,2},{9,3},... | collective-permute-start | bytes 294920 | tf_op jit(solution)/shard_map/ppermute | solution.py:267
  88.5 1.3 %collective-permute-start.40 = (bf16[128,384]{1,0:T(8,128)(2,1)}, bf16[128,384]{1,0:T(8,128)(2,1)S(1)}, u32[]{:S(2)}, u32[]{:S(2)}) collective-permute-start(bf16[128,384]{1,0:T(8,128)(2,1)} %get-tuple-element.53), channel_id=1, source_target_pairs={{0,11},{1,10},{2,9},{3,8},{4,15},{5,14},{6,13},{7,12},{8,3},{9,2},... | collective-permute-start | bytes 294920 | tf_op jit(solution)/shard_map/ppermute | solution.py:267
  90.1 8.3 %all-to-all-done.refs_32_ = bf16[16,128,384]{2,1,0:T(8,128)(2,1)} async-done(((bf16[16,128,384]{2,1,0:T(8,128)(2,1)}), bf16[16,128,384]{2,1,0:T(8,128)(2,1)}, u32[]{:S(2)}, u32[]{:S(2)}) %all-to-all-start) | async-done | bytes 1572896 | tf_op jit(solution)/shard_map/all_to_all | solution.py:306
  98.5 10.4 %grad_w.1 = bf16[384,2048]{1,0:T(8,128)(2,1)} custom-call(s32[16]{0:T(128)} %get-tuple-element.67.ids_ref, bf16[64,2048]{1,0:T(8,128)(2,1)} %copy-done.3, bf16[64,2048]{1,0:T(8,128)(2,1)} %copy-done.2, bf16[64,2048]{1,0:T(8,128)(2,1)} %copy-done.13, bf16[64,2048]{1,0:T(8,128)(2,1)} %copy-done.12, bf16[64,2048]{1,0:T(8,128)(2,1)} %copy-done.6, ...), custom_call_target="tpu_custom_call" | custom-call | flops 3221225472 | bytes 11534336 | tf_op jit(solution)/shard_map/grad_w/pallas_call | solution.py:334
  109.4 8.3 %collective-permute-done.42.refs_13_ = bf16[128,384]{1,0:T(8,128)(2,1)S(1)} collective-permute-done((bf16[128,384]{1,0:T(8,128)(2,1)S(1)}, bf16[128,384]{1,0:T(8,128)(2,1)S(1)}, u32[]{:S(2)}, u32[]{:S(2)}) %collective-permute-start.42) | collective-permute-done | bytes 98336 | tf_op jit(solution)/shard_map/ppermute | solution.py:267
  118.7 2.3 %collective-permute-done.44.refs_15_ = bf16[128,384]{1,0:T(8,128)(2,1)S(1)} collective-permute-done((bf16[128,384]{1,0:T(8,128)(2,1)S(1)}, bf16[128,384]{1,0:T(8,128)(2,1)S(1)}, u32[]{:S(2)}, u32[]{:S(2)}) %collective-permute-start.44) | collective-permute-done | bytes 98336 | tf_op jit(solution)/shard_map/ppermute | solution.py:267
  121.0 2.8 %combine.1 = (bf16[1024,384]{1,0:T(8,128)(2,1)}, bf16[8,128]{1,0:T(8,128)(2,1)}) custom-call(s32[8,128]{1,0:T(8,128)S(1)} %reshape.21.routes_ref, bf16[8,128]{1,0:T(8,128)(2,1)S(1)} %reshape.22.probs_ref, bf16[1024,384]{1,0:T(8,128)(2,1)S(1)} %bitcast.10, bf16[128,384]{1,0:T(8,128)(2,1)S(1)} %copy-done.1, ...), custom_call_target="tpu_custom_call" | custom-call | tf_op jit(solution)/shard_map/combine/pallas_call | solution.py:360
  (139 shorter events, 23.9 us)
Async XLA Ops:
  3.3 12.3 %collective-permute-start.3 = (bf16[64,2048]{1,0:T(8,128)(2,1)S(1)}, bf16[64,2048]{1,0:T(8,128)(2,1)S(1)}, u32[]{:S(2)}, u32[]{:S(2)}) collective-permute-start(bf16[64,2048]{1,0:T(8,128)(2,1)S(1)} %get-tuple-element.65.refs_1_), channel_id=1, source_target_pairs={{0,4},{1,5},{2,0},{3,1},{4,8},{5,9},{6,2},{7,3},{8,12},{9,13},{10,... | collective-permute-start | bytes 786440 | tf_op jit(solution)/shard_map/ppermute | solution.py:235
  3.5 12.3 %collective-permute-start.6 = (bf16[64,2048]{1,0:T(8,128)(2,1)S(1)}, bf16[64,2048]{1,0:T(8,128)(2,1)S(1)}, u32[]{:S(2)}, u32[]{:S(2)}) collective-permute-start(bf16[64,2048]{1,0:T(8,128)(2,1)S(1)} %get-tuple-element.66.refs_0_), channel_id=1, source_target_pairs={{4,0},{5,1},{0,2},{1,3},{8,4},{9,5},{2,6},{3,7},{12,8},{13,9},{6,1... | collective-permute-start | bytes 786440 | tf_op jit(solution)/shard_map/ppermute | solution.py:236
  9.0 11.2 %collective-permute-start.15 = (bf16[64,2048]{1,0:T(8,128)(2,1)S(1)}, bf16[64,2048]{1,0:T(8,128)(2,1)S(1)}, u32[]{:S(2)}, u32[]{:S(2)}) collective-permute-start(bf16[64,2048]{1,0:T(8,128)(2,1)S(1)} %collective-permute-done.7.refs_9_), channel_id=1, source_target_pairs={{4,0},{5,1},{0,2},{1,3},{8,4},{9,5},{2,6},{3,7},{12,8},{13,9},{6,1... | collective-permute-start | bytes 786440 | tf_op jit(solution)/shard_map/ppermute | solution.py:234
  10.3 11.2 %collective-permute-start.10 = (bf16[64,2048]{1,0:T(8,128)(2,1)S(1)}, bf16[64,2048]{1,0:T(8,128)(2,1)S(1)}, u32[]{:S(2)}, u32[]{:S(2)}) collective-permute-start(bf16[64,2048]{1,0:T(8,128)(2,1)S(1)} %collective-permute-done.2.refs_4_), channel_id=1, source_target_pairs={{0,4},{1,5},{2,0},{3,1},{4,8},{5,9},{6,2},{7,3},{8,12},{9,13},{10,... | collective-permute-start | bytes 786440 | tf_op jit(solution)/shard_map/ppermute | solution.py:233
  15.6 11.3 %collective-permute-start.11 = (bf16[64,2048]{1,0:T(8,128)(2,1)S(1)}, bf16[64,2048]{1,0:T(8,128)(2,1)S(1)}, u32[]{:S(2)}, u32[]{:S(2)}) collective-permute-start(bf16[64,2048]{1,0:T(8,128)(2,1)S(1)} %collective-permute-done.3.refs_5_), channel_id=1, source_target_pairs={{0,4},{1,5},{2,0},{3,1},{4,8},{5,9},{6,2},{7,3},{8,12},{9,13},{10,... | collective-permute-start | bytes 786440 | tf_op jit(solution)/shard_map/ppermute | solution.py:235
  15.8 11.3 %collective-permute-start.14 = (bf16[64,2048]{1,0:T(8,128)(2,1)S(1)}, bf16[64,2048]{1,0:T(8,128)(2,1)}, u32[]{:S(2)}, u32[]{:S(2)}) collective-permute-start(bf16[64,2048]{1,0:T(8,128)(2,1)S(1)} %collective-permute-done.6.refs_8_), channel_id=1, source_target_pairs={{4,0},{5,1},{0,2},{1,3},{8,4},{9,5},{2,6},{3,7},{12,8},{13,9},{6,1... | collective-permute-start | bytes 786440 | tf_op jit(solution)/shard_map/ppermute | solution.py:236
  20.3 11.3 %collective-permute-start.23 = (bf16[64,2048]{1,0:T(8,128)(2,1)S(1)}, bf16[64,2048]{1,0:T(8,128)(2,1)}, u32[]{:S(2)}, u32[]{:S(2)}) collective-permute-start(bf16[64,2048]{1,0:T(8,128)(2,1)S(1)} %collective-permute-done.15.refs_17_), channel_id=1, source_target_pairs={{4,0},{5,1},{0,2},{1,3},{8,4},{9,5},{2,6},{3,7},{12,8},{13,9},{6,1... | collective-permute-start | bytes 786440 | tf_op jit(solution)/shard_map/ppermute | solution.py:234
  21.6 11.3 %collective-permute-start.18 = (bf16[64,2048]{1,0:T(8,128)(2,1)S(1)}, bf16[64,2048]{1,0:T(8,128)(2,1)}, u32[]{:S(2)}, u32[]{:S(2)}) collective-permute-start(bf16[64,2048]{1,0:T(8,128)(2,1)S(1)} %collective-permute-done.10.refs_12_), channel_id=1, source_target_pairs={{0,4},{1,5},{2,0},{3,1},{4,8},{5,9},{6,2},{7,3},{8,12},{9,13},{10,... | collective-permute-start | bytes 786440 | tf_op jit(solution)/shard_map/ppermute | solution.py:233
  27.0 11.2 %collective-permute-start.19 = (bf16[64,2048]{1,0:T(8,128)(2,1)S(1)}, bf16[64,2048]{1,0:T(8,128)(2,1)}, u32[]{:S(2)}, u32[]{:S(2)}) collective-permute-start(bf16[64,2048]{1,0:T(8,128)(2,1)S(1)} %collective-permute-done.11.refs_13_), channel_id=1, source_target_pairs={{0,4},{1,5},{2,0},{3,1},{4,8},{5,9},{6,2},{7,3},{8,12},{9,13},{10,... | collective-permute-start | bytes 786440 | tf_op jit(solution)/shard_map/ppermute | solution.py:235
  27.1 11.1 %collective-permute-start.22 = (bf16[64,2048]{1,0:T(8,128)(2,1)}, bf16[64,2048]{1,0:T(8,128)(2,1)}, u32[]{:S(2)}, u32[]{:S(2)}) collective-permute-start(bf16[64,2048]{1,0:T(8,128)(2,1)} %collective-permute-done.14.refs_16_), channel_id=1, source_target_pairs={{4,0},{5,1},{0,2},{1,3},{8,4},{9,5},{2,6},{3,7},{12,8},{13,9},{6,1... | collective-permute-start | bytes 786440 | tf_op jit(solution)/shard_map/ppermute | solution.py:236
  31.5 11.0 %collective-permute-start.27 = (bf16[64,2048]{1,0:T(8,128)(2,1)}, bf16[64,2048]{1,0:T(8,128)(2,1)}, u32[]{:S(2)}, u32[]{:S(2)}) collective-permute-start(bf16[64,2048]{1,0:T(8,128)(2,1)} %collective-permute-done.23.refs_25_), channel_id=1, source_target_pairs={{4,0},{5,1},{0,2},{1,3},{8,4},{9,5},{2,6},{3,7},{12,8},{13,9},{6,1... | collective-permute-start | bytes 786440 | tf_op jit(solution)/shard_map/ppermute | solution.py:244
  32.8 11.0 %collective-permute-start.26 = (bf16[64,2048]{1,0:T(8,128)(2,1)}, bf16[64,2048]{1,0:T(8,128)(2,1)}, u32[]{:S(2)}, u32[]{:S(2)}) collective-permute-start(bf16[64,2048]{1,0:T(8,128)(2,1)} %collective-permute-done.18.refs_20_), channel_id=1, source_target_pairs={{0,4},{1,5},{2,0},{3,1},{4,8},{5,9},{6,2},{7,3},{8,12},{9,13},{10,... | collective-permute-start | bytes 786440 | tf_op jit(solution)/shard_map/ppermute | solution.py:243
  43.8 54.6 %all-to-all-start = ((bf16[16,128,384]{2,1,0:T(8,128)(2,1)}), bf16[16,128,384]{2,1,0:T(8,128)(2,1)}, u32[]{:S(2)}, u32[]{:S(2)}) async-start(bf16[16,128,384]{2,1,0:T(8,128)(2,1)} %dispatch.1), calls=%async_computation | async-start | bytes 3145728 | tf_op jit(solution)/shard_map/all_to_all | solution.py:306
  68.7 11.1 %collective-permute-start.32 = (bf16[128,384]{1,0:T(8,128)(2,1)}, bf16[128,384]{1,0:T(8,128)(2,1)S(1)}, u32[]{:S(2)}, u32[]{:S(2)}) collective-permute-start(bf16[128,384]{1,0:T(8,128)(2,1)} %get-tuple-element.38), channel_id=1, source_target_pairs={{0,3},{1,2},{2,1},{3,0},{4,7},{5,6},{6,5},{7,4},{8,11},{9,10},{10,... | collective-permute-start | bytes 294920 | tf_op jit(solution)/shard_map/ppermute | solution.py:267
  70.7 11.7 %collective-permute-start.34 = (bf16[128,384]{1,0:T(8,128)(2,1)}, bf16[128,384]{1,0:T(8,128)(2,1)S(1)}, u32[]{:S(2)}, u32[]{:S(2)}) collective-permute-start(bf16[128,384]{1,0:T(8,128)(2,1)} %get-tuple-element.40), channel_id=1, source_target_pairs={{0,5},{1,4},{2,7},{3,6},{4,1},{5,0},{6,3},{7,2},{8,13},{9,12},{10,... | collective-permute-start | bytes 294920 | tf_op jit(solution)/shard_map/ppermute | solution.py:267
  71.9 16.5 %collective-permute-start.35 = (bf16[128,384]{1,0:T(8,128)(2,1)}, bf16[128,384]{1,0:T(8,128)(2,1)S(1)}, u32[]{:S(2)}, u32[]{:S(2)}) collective-permute-start(bf16[128,384]{1,0:T(8,128)(2,1)} %get-tuple-element.41), channel_id=1, source_target_pairs={{0,6},{1,7},{2,4},{3,5},{4,2},{5,3},{6,0},{7,1},{8,14},{9,15},{10,... | collective-permute-start | bytes 294920 | tf_op jit(solution)/shard_map/ppermute | solution.py:267
  72.7 17.0 %collective-permute-start.36 = (bf16[128,384]{1,0:T(8,128)(2,1)}, bf16[128,384]{1,0:T(8,128)(2,1)S(1)}, u32[]{:S(2)}, u32[]{:S(2)}) collective-permute-start(bf16[128,384]{1,0:T(8,128)(2,1)} %get-tuple-element.42), channel_id=1, source_target_pairs={{0,7},{1,6},{2,5},{3,4},{4,3},{5,2},{6,1},{7,0},{8,15},{9,14},{10,... | collective-permute-start | bytes 294920 | tf_op jit(solution)/shard_map/ppermute | solution.py:267
  79.7 29.1 %collective-permute-start.37 = (bf16[128,384]{1,0:T(8,128)(2,1)}, bf16[128,384]{1,0:T(8,128)(2,1)S(1)}, u32[]{:S(2)}, u32[]{:S(2)}) collective-permute-start(bf16[128,384]{1,0:T(8,128)(2,1)} %get-tuple-element.50), channel_id=1, source_target_pairs={{0,8},{1,9},{2,10},{3,11},{4,12},{5,13},{6,14},{7,15},{8,0},{9,1},... | collective-permute-start | bytes 294920 | tf_op jit(solution)/shard_map/ppermute | solution.py:267
  79.8 29.2 %collective-permute-start.38 = (bf16[128,384]{1,0:T(8,128)(2,1)}, bf16[128,384]{1,0:T(8,128)(2,1)S(1)}, u32[]{:S(2)}, u32[]{:S(2)}) collective-permute-start(bf16[128,384]{1,0:T(8,128)(2,1)} %get-tuple-element.51), channel_id=1, source_target_pairs={{0,9},{1,8},{2,11},{3,10},{4,13},{5,12},{6,15},{7,14},{8,1},{9,0},... | collective-permute-start | bytes 294920 | tf_op jit(solution)/shard_map/ppermute | solution.py:267
  82.4 26.6 %collective-permute-start.39 = (bf16[128,384]{1,0:T(8,128)(2,1)}, bf16[128,384]{1,0:T(8,128)(2,1)S(1)}, u32[]{:S(2)}, u32[]{:S(2)}) collective-permute-start(bf16[128,384]{1,0:T(8,128)(2,1)} %get-tuple-element.52), channel_id=1, source_target_pairs={{0,10},{1,11},{2,8},{3,9},{4,14},{5,15},{6,12},{7,13},{8,2},{9,3},... | collective-permute-start | bytes 294920 | tf_op jit(solution)/shard_map/ppermute | solution.py:267
  88.5 20.9 %collective-permute-start.40 = (bf16[128,384]{1,0:T(8,128)(2,1)}, bf16[128,384]{1,0:T(8,128)(2,1)S(1)}, u32[]{:S(2)}, u32[]{:S(2)}) collective-permute-start(bf16[128,384]{1,0:T(8,128)(2,1)} %get-tuple-element.53), channel_id=1, source_target_pairs={{0,11},{1,10},{2,9},{3,8},{4,15},{5,14},{6,13},{7,12},{8,3},{9,2},... | collective-permute-start | bytes 294920 | tf_op jit(solution)/shard_map/ppermute | solution.py:267
  89.8 19.6 %collective-permute-start.41 = (bf16[128,384]{1,0:T(8,128)(2,1)}, bf16[128,384]{1,0:T(8,128)(2,1)S(1)}, u32[]{:S(2)}, u32[]{:S(2)}) collective-permute-start(bf16[128,384]{1,0:T(8,128)(2,1)} %get-tuple-element.54), channel_id=1, source_target_pairs={{0,12},{1,13},{2,14},{3,15},{4,8},{5,9},{6,10},{7,11},{8,4},{9,5},... | collective-permute-start | bytes 294920 | tf_op jit(solution)/shard_map/ppermute | solution.py:267
  108.9 9.8 %collective-permute-start.43 = (bf16[128,384]{1,0:T(8,128)(2,1)S(1)}, bf16[128,384]{1,0:T(8,128)(2,1)S(1)}, u32[]{:S(2)}, u32[]{:S(2)}) collective-permute-start(bf16[128,384]{1,0:T(8,128)(2,1)S(1)} %copy-done.27), channel_id=1, source_target_pairs={{0,14},{1,15},{2,12},{3,13},{4,10},{5,11},{6,8},{7,9},{8,6},{9,7},... | collective-permute-start | bytes 294920 | tf_op jit(solution)/shard_map/ppermute | solution.py:267
  109.0 12.0 %collective-permute-start.44 = (bf16[128,384]{1,0:T(8,128)(2,1)S(1)}, bf16[128,384]{1,0:T(8,128)(2,1)S(1)}, u32[]{:S(2)}, u32[]{:S(2)}) collective-permute-start(bf16[128,384]{1,0:T(8,128)(2,1)S(1)} %copy-done.26), channel_id=1, source_target_pairs={{0,15},{1,14},{2,13},{3,12},{4,11},{5,10},{6,9},{7,8},{8,7},{9,6},... | collective-permute-start | bytes 294920 | tf_op jit(solution)/shard_map/ppermute | solution.py:267
  (51 other events, 553.8 us)

commit v4 on v3

--- a/solution.py
+++ b/solution.py
@@ -120,11 +120,9 @@
     span = GROUP * top_count
     inner_width = hidden_ref.shape[1]
     ones = jnp.ones((top_count, inner_width), jnp.bfloat16)
-    summed = jnp.zeros(prob_ref.shape, jnp.float32)
+    totals = []
     row = lax.broadcasted_iota(jnp.int32, (top_count, span), 0)
     col = lax.broadcasted_iota(jnp.int32, (top_count, span), 1)
-    slot = lax.broadcasted_iota(jnp.int32, (span, prob_ref.shape[1]), 0)
-    token = lax.broadcasted_iota(jnp.int32, (span, prob_ref.shape[1]), 1)
     across = (((0,), (0,)), ((), ()))
     lanes = (((1,), (1,)), ((), ()))
     for g in range(routes_ref.shape[0]):
@@ -139,14 +137,16 @@
             scaled.astype(jnp.bfloat16), block, across, preferred_element_type=jnp.float32
         ).astype(jnp.bfloat16)
         product = mine * hidden_ref[g * span : (g + 1) * span, :].astype(jnp.float32)
-        high = product.astype(jnp.bfloat16)
-        low = (product - high.astype(jnp.float32)).astype(jnp.bfloat16)
-        total = lax.dot_general(ones, high, lanes, preferred_element_type=jnp.float32)
-        total += lax.dot_general(ones, low, lanes, preferred_element_type=jnp.float32)
-        own = jnp.where(col % top_count == row, total, 0.0).astype(jnp.bfloat16)
-        to_token = jnp.where(token == slot // top_count + g * GROUP, 1.0, 0.0)
-        summed += jnp.dot(own, to_token.astype(jnp.bfloat16), preferred_element_type=jnp.float32)
-    prob_ref[...] = summed.astype(jnp.bfloat16)
+        part = product[:, :span]
+        for first in range(span, inner_width, span):
+            part += product[:, first : first + span]
+        total = jnp.sum(part.T, axis=0, keepdims=True)
+        totals.append(jnp.where(col % top_count == row, total, 0.0).astype(jnp.bfloat16))
+    totals = jnp.concatenate(totals, axis=1)
+    slot = lax.broadcasted_iota(jnp.int32, (totals.shape[1], prob_ref.shape[1]), 0)
+    token = lax.broadcasted_iota(jnp.int32, slot.shape, 1)
+    to_token = jnp.where(token == slot // top_count, 1.0, 0.0).astype(jnp.bfloat16)
+    prob_ref[...] = jnp.dot(totals, to_token, preferred_element_type=jnp.float32).astype(jnp.bfloat16)
 
 
 def back_kernel(order_ref, *refs, places, step, block):
@@ -323,10 +323,10 @@
         ),
         name="back_rows",
     )(order, *pieces, local_weight)
-    held_back = range(peer_count - 3, peer_count)
+    held_back = range(peer_count - 2, peer_count)
     got_back = {0: back[0]} | exchange(back, [k for k in range(1, peer_count) if k not in held_back])
 
-    near = {k: got_back[k] for k in range(1, peer_count // 2)}
+    near = {k: got_back[k] for k in range(1, peer_count // 2) if k in got_back}
     got_hidden, near = lax.optimization_barrier((got_hidden, near))
     got_back |= near
     width = model_width // SPLIT
@@ -385,7 +385,8 @@
         and peer_count % 4 == 0
         and peer_count & (peer_count - 1) == 0
         and token_count % (2 * GROUP) == 0
-        and (GROUP * top_count) % 128 == 0
+        and GROUP * top_count == 128
+        and hidden.shape[2] % 128 == 0
     )
     body = dense_on_device if dense else padded_on_device
     return body(grad_out, hidden, routes, probs, w_down)

time: 125 us -> 124 us (level)
  transfers between devices with their start and end apart: 46 -> 46, of which waited for: 19 -> 19; matrix products, arithmetic and copies ran while one was open for 3% -> 3% of each run, Pallas kernels for 17% -> 18%
where the time goes in v4:
time: 124 us; the launch traced here: 123 us
  waiting for transfers between devices  54.1 us (44%)
  starting transfers between devices  39.5 us (32%)
  Pallas kernels  23.2 us (19%)
  local copies, waits for them, and re-layouts  5 us (4%)
    ppermute x15, starting transfers between devices, exchange(): lax.ppermute(blocks[k], 'expert', [(i, i ^ k) for i in peers])  17.2 us
    ppermute x15, waiting for transfers between devices, exchange(): lax.ppermute(blocks[k], 'expert', [(i, i ^ k) for i in peers])  16.7 us
    ppermute x3, waiting for transfers between devices, gather_round(): high_fore = lax.ppermute(high_fore, 'expert', ahead)  12.1 us
    ppermute x3, waiting for transfers between devices, gather_round(): high_aft = lax.ppermute(high_aft, 'expert', behind)  10.5 us
    pallas_call x1, Pallas kernels, dense_on_device(): pl.pallas_call(functools.partial(weight_kernel, places=places, first_col=...  10.4 us
    pallas_call x1, Pallas kernels, dense_on_device(): pl.pallas_call(functools.partial(back_kernel, places=places, step=4 * tok...  9.49 us
    all_to_all x1, waiting for transfers between devices, dense_on_device(): lax.all_to_all(sent, 'expert', split_axis=0, concat_axis=0, tiled=True)  8.31 us
    all_to_all x1, starting transfers between devices, dense_on_device(): lax.all_to_all(sent, 'expert', split_axis=0, concat_axis=0, tiled=True)  6.73 us
  transfers between devices with their start and end apart: 46, of which 19 were waited for; matrix products, arithmetic and copies ran while one was open for 3% of the time, Pallas kernels for 18%

profile of v4, /device:TPU:15, one launch (start us, length us, event | category | flops | bytes accessed | tf_op | source)
XLA Modules:
  0.0 122.7 jit_solution(17379360384768324687)
XLA Ops:
  1.8 1.3 %collective-permute-start.7 = (bf16[64,2048]{1,0:T(8,128)(2,1)S(1)}, bf16[64,2048]{1,0:T(8,128)(2,1)S(1)}, u32[]{:S(2)}, u32[]{:S(2)}) collective-permute-start(bf16[64,2048]{1,0:T(8,128)(2,1)S(1)} %get-tuple-element.63.refs_1_), channel_id=1, source_target_pairs={{4,0},{5,1},{0,2},{1,3},{8,4},{9,5},{2,6},{3,7},{12,8},{13,9},{6,1... | collective-permute-start | bytes 786440 | tf_op jit(solution)/shard_map/ppermute | solution.py:234
  4.8 4.2 %collective-permute-done.7.refs_9_ = bf16[64,2048]{1,0:T(8,128)(2,1)S(1)} collective-permute-done((bf16[64,2048]{1,0:T(8,128)(2,1)S(1)}, bf16[64,2048]{1,0:T(8,128)(2,1)S(1)}, u32[]{:S(2)}, u32[]{:S(2)}) %collective-permute-start.7) | collective-permute-done | bytes 262176 | tf_op jit(solution)/shard_map/ppermute | solution.py:234
  10.5 5.1 %collective-permute-done.3.refs_5_ = bf16[64,2048]{1,0:T(8,128)(2,1)S(1)} collective-permute-done((bf16[64,2048]{1,0:T(8,128)(2,1)S(1)}, bf16[64,2048]{1,0:T(8,128)(2,1)S(1)}, u32[]{:S(2)}, u32[]{:S(2)}) %collective-permute-start.3) | collective-permute-done | bytes 262176 | tf_op jit(solution)/shard_map/ppermute | solution.py:235
  15.8 1.3 %collective-permute-start.14 = (bf16[64,2048]{1,0:T(8,128)(2,1)S(1)}, bf16[64,2048]{1,0:T(8,128)(2,1)}, u32[]{:S(2)}, u32[]{:S(2)}) collective-permute-start(bf16[64,2048]{1,0:T(8,128)(2,1)S(1)} %collective-permute-done.6.refs_8_), channel_id=1, source_target_pairs={{4,0},{5,1},{0,2},{1,3},{8,4},{9,5},{2,6},{3,7},{12,8},{13,9},{6,1... | collective-permute-start | bytes 786440 | tf_op jit(solution)/shard_map/ppermute | solution.py:236
  17.1 3.2 %collective-permute-done.15.refs_17_ = bf16[64,2048]{1,0:T(8,128)(2,1)S(1)} collective-permute-done((bf16[64,2048]{1,0:T(8,128)(2,1)S(1)}, bf16[64,2048]{1,0:T(8,128)(2,1)S(1)}, u32[]{:S(2)}, u32[]{:S(2)}) %collective-permute-start.15) | collective-permute-done | bytes 262176 | tf_op jit(solution)/shard_map/ppermute | solution.py:234
  21.7 5.2 %collective-permute-done.11.refs_13_ = bf16[64,2048]{1,0:T(8,128)(2,1)S(1)} collective-permute-done((bf16[64,2048]{1,0:T(8,128)(2,1)S(1)}, bf16[64,2048]{1,0:T(8,128)(2,1)S(1)}, u32[]{:S(2)}, u32[]{:S(2)}) %collective-permute-start.11) | collective-permute-done | bytes 262176 | tf_op jit(solution)/shard_map/ppermute | solution.py:235
  27.1 1.3 %collective-permute-start.22 = (bf16[64,2048]{1,0:T(8,128)(2,1)}, bf16[64,2048]{1,0:T(8,128)(2,1)}, u32[]{:S(2)}, u32[]{:S(2)}) collective-permute-start(bf16[64,2048]{1,0:T(8,128)(2,1)} %collective-permute-done.14.refs_16_), channel_id=1, source_target_pairs={{4,0},{5,1},{0,2},{1,3},{8,4},{9,5},{2,6},{3,7},{12,8},{13,9},{6,1... | collective-permute-start | bytes 786440 | tf_op jit(solution)/shard_map/ppermute | solution.py:236
  28.4 3.1 %collective-permute-done.23.refs_25_ = bf16[64,2048]{1,0:T(8,128)(2,1)} collective-permute-done((bf16[64,2048]{1,0:T(8,128)(2,1)S(1)}, bf16[64,2048]{1,0:T(8,128)(2,1)}, u32[]{:S(2)}, u32[]{:S(2)}) %collective-permute-start.23) | collective-permute-done | bytes 262176 | tf_op jit(solution)/shard_map/ppermute | solution.py:234
  34.8 1.7 %dispatch.1 = bf16[16,128,384]{2,1,0:T(8,128)(2,1)} custom-call(s32[8,128]{1,0:T(8,128)S(1)} %reshape.24.routes_ref, bf16[8,128]{1,0:T(8,128)(2,1)S(1)} %reshape.22.probs_ref, bf16[1024,384]{1,0:T(8,128)(2,1)S(1)} %bitcast.9), custom_call_target="tpu_custom_call" | custom-call | tf_op jit(solution)/shard_map/dispatch/pallas_call | solution.py:297
  36.5 1.7 %collective-permute-done.19.refs_21_ = bf16[64,2048]{1,0:T(8,128)(2,1)} collective-permute-done((bf16[64,2048]{1,0:T(8,128)(2,1)S(1)}, bf16[64,2048]{1,0:T(8,128)(2,1)}, u32[]{:S(2)}, u32[]{:S(2)}) %collective-permute-start.19) | collective-permute-done | bytes 262176 | tf_op jit(solution)/shard_map/ppermute | solution.py:235
  38.2 4.3 %collective-permute-done.27.refs_29_ = bf16[64,2048]{1,0:T(8,128)(2,1)} collective-permute-done((bf16[64,2048]{1,0:T(8,128)(2,1)}, bf16[64,2048]{1,0:T(8,128)(2,1)}, u32[]{:S(2)}, u32[]{:S(2)}) %collective-permute-start.27) | collective-permute-done | bytes 262176 | tf_op jit(solution)/shard_map/ppermute | solution.py:244
  43.8 6.7 %all-to-all-start = ((bf16[16,128,384]{2,1,0:T(8,128)(2,1)}), bf16[16,128,384]{2,1,0:T(8,128)(2,1)}, u32[]{:S(2)}, u32[]{:S(2)}) async-start(bf16[16,128,384]{2,1,0:T(8,128)(2,1)} %dispatch.1), calls=%async_computation | async-start | bytes 3145728 | tf_op jit(solution)/shard_map/all_to_all | solution.py:306
  58.7 9.5 %back_rows.1 = (bf16[128,384]{1,0:T(8,128)(2,1)}, bf16[128,384]{1,0:T(8,128)(2,1)}, bf16[128,384]{1,0:T(8,128)(2,1)}, bf16[128,384]{1,0:T(8,128)(2,1)}, bf16[128...) custom-call(s32[16]{0:T(128)} %get-tuple-element.66.order_ref, ...), custom_call_target="tpu_custom_call" | custom-call | flops 3221225472 | bytes 9961472 | tf_op jit(solution)/shard_map/back_rows/pallas_call | solution.py:308
  68.7 1.7 %collective-permute-start.32 = (bf16[128,384]{1,0:T(8,128)(2,1)}, bf16[128,384]{1,0:T(8,128)(2,1)S(1)}, u32[]{:S(2)}, u32[]{:S(2)}) collective-permute-start(bf16[128,384]{1,0:T(8,128)(2,1)} %get-tuple-element.37), channel_id=1, source_target_pairs={{0,3},{1,2},{2,1},{3,0},{4,7},{5,6},{6,5},{7,4},{8,11},{9,10},{10,... | collective-permute-start | bytes 294920 | tf_op jit(solution)/shard_map/ppermute | solution.py:267
  72.7 3.1 %collective-permute-start.36 = (bf16[128,384]{1,0:T(8,128)(2,1)}, bf16[128,384]{1,0:T(8,128)(2,1)S(1)}, u32[]{:S(2)}, u32[]{:S(2)}) collective-permute-start(bf16[128,384]{1,0:T(8,128)(2,1)} %get-tuple-element.41), channel_id=1, source_target_pairs={{0,7},{1,6},{2,5},{3,4},{4,3},{5,2},{6,1},{7,0},{8,15},{9,14},{10,... | collective-permute-start | bytes 294920 | tf_op jit(solution)/shard_map/ppermute | solution.py:267
  75.9 3.9 %collective-permute-done.32.refs_3_ = bf16[128,384]{1,0:T(8,128)(2,1)S(1)} collective-permute-done((bf16[128,384]{1,0:T(8,128)(2,1)}, bf16[128,384]{1,0:T(8,128)(2,1)S(1)}, u32[]{:S(2)}, u32[]{:S(2)}) %collective-permute-start.32) | collective-permute-done | bytes 98336 | tf_op jit(solution)/shard_map/ppermute | solution.py:267
  79.8 2.2 %collective-permute-start.38 = (bf16[128,384]{1,0:T(8,128)(2,1)}, bf16[128,384]{1,0:T(8,128)(2,1)S(1)}, u32[]{:S(2)}, u32[]{:S(2)}) collective-permute-start(bf16[128,384]{1,0:T(8,128)(2,1)} %get-tuple-element.50), channel_id=1, source_target_pairs={{0,9},{1,8},{2,11},{3,10},{4,13},{5,12},{6,15},{7,14},{8,1},{9,0},... | collective-permute-start | bytes 294920 | tf_op jit(solution)/shard_map/ppermute | solution.py:267
  82.4 6.0 %collective-permute-start.39 = (bf16[128,384]{1,0:T(8,128)(2,1)}, bf16[128,384]{1,0:T(8,128)(2,1)S(1)}, u32[]{:S(2)}, u32[]{:S(2)}) collective-permute-start(bf16[128,384]{1,0:T(8,128)(2,1)} %get-tuple-element.51), channel_id=1, source_target_pairs={{0,10},{1,11},{2,8},{3,9},{4,14},{5,15},{6,12},{7,13},{8,2},{9,3},... | collective-permute-start | bytes 294920 | tf_op jit(solution)/shard_map/ppermute | solution.py:267
  88.5 1.3 %collective-permute-start.40 = (bf16[128,384]{1,0:T(8,128)(2,1)}, bf16[128,384]{1,0:T(8,128)(2,1)S(1)}, u32[]{:S(2)}, u32[]{:S(2)}) collective-permute-start(bf16[128,384]{1,0:T(8,128)(2,1)} %get-tuple-element.52), channel_id=1, source_target_pairs={{0,11},{1,10},{2,9},{3,8},{4,15},{5,14},{6,13},{7,12},{8,3},{9,2},... | collective-permute-start | bytes 294920 | tf_op jit(solution)/shard_map/ppermute | solution.py:267
  90.1 8.3 %all-to-all-done.refs_32_ = bf16[16,128,384]{2,1,0:T(8,128)(2,1)} async-done(((bf16[16,128,384]{2,1,0:T(8,128)(2,1)}), bf16[16,128,384]{2,1,0:T(8,128)(2,1)}, u32[]{:S(2)}, u32[]{:S(2)}) %all-to-all-start) | async-done | bytes 1572896 | tf_op jit(solution)/shard_map/all_to_all | solution.py:306
  98.5 10.4 %grad_w.1 = bf16[384,2048]{1,0:T(8,128)(2,1)} custom-call(s32[16]{0:T(128)} %get-tuple-element.65.ids_ref, bf16[64,2048]{1,0:T(8,128)(2,1)} %copy-done.3, bf16[64,2048]{1,0:T(8,128)(2,1)} %copy-done.2, bf16[64,2048]{1,0:T(8,128)(2,1)} %copy-done.13, bf16[64,2048]{1,0:T(8,128)(2,1)} %copy-done.12, bf16[64,2048]{1,0:T(8,128)(2,1)} %copy-done.6, ...), custom_call_target="tpu_custom_call" | custom-call | flops 3221225472 | bytes 11534336 | tf_op jit(solution)/shard_map/grad_w/pallas_call | solution.py:334
  109.4 8.3 %collective-permute-done.42.refs_13_ = bf16[128,384]{1,0:T(8,128)(2,1)S(1)} collective-permute-done((bf16[128,384]{1,0:T(8,128)(2,1)S(1)}, bf16[128,384]{1,0:T(8,128)(2,1)S(1)}, u32[]{:S(2)}, u32[]{:S(2)}) %collective-permute-start.42) | collective-permute-done | bytes 98336 | tf_op jit(solution)/shard_map/ppermute | solution.py:267
  118.7 2.3 %collective-permute-done.44.refs_15_ = bf16[128,384]{1,0:T(8,128)(2,1)S(1)} collective-permute-done((bf16[128,384]{1,0:T(8,128)(2,1)S(1)}, bf16[128,384]{1,0:T(8,128)(2,1)S(1)}, u32[]{:S(2)}, u32[]{:S(2)}) %collective-permute-start.44) | collective-permute-done | bytes 98336 | tf_op jit(solution)/shard_map/ppermute | solution.py:267
  121.0 1.7 %combine.1 = (bf16[1024,384]{1,0:T(8,128)(2,1)}, bf16[8,128]{1,0:T(8,128)(2,1)}) custom-call(s32[8,128]{1,0:T(8,128)S(1)} %reshape.21.routes_ref, bf16[8,128]{1,0:T(8,128)(2,1)S(1)} %reshape.22.probs_ref, bf16[1024,384]{1,0:T(8,128)(2,1)S(1)} %bitcast.10, bf16[128,384]{1,0:T(8,128)(2,1)S(1)} %copy-done.1, ...), custom_call_target="tpu_custom_call" | custom-call | tf_op jit(solution)/shard_map/combine/pallas_call | solution.py:360
  (139 shorter events, 23.9 us)
Async XLA Ops:
  3.3 12.3 %collective-permute-start.3 = (bf16[64,2048]{1,0:T(8,128)(2,1)S(1)}, bf16[64,2048]{1,0:T(8,128)(2,1)S(1)}, u32[]{:S(2)}, u32[]{:S(2)}) collective-permute-start(bf16[64,2048]{1,0:T(8,128)(2,1)S(1)} %get-tuple-element.63.refs_1_), channel_id=1, source_target_pairs={{0,4},{1,5},{2,0},{3,1},{4,8},{5,9},{6,2},{7,3},{8,12},{9,13},{10,... | collective-permute-start | bytes 786440 | tf_op jit(solution)/shard_map/ppermute | solution.py:235
  3.5 12.3 %collective-permute-start.6 = (bf16[64,2048]{1,0:T(8,128)(2,1)S(1)}, bf16[64,2048]{1,0:T(8,128)(2,1)S(1)}, u32[]{:S(2)}, u32[]{:S(2)}) collective-permute-start(bf16[64,2048]{1,0:T(8,128)(2,1)S(1)} %get-tuple-element.64.refs_0_), channel_id=1, source_target_pairs={{4,0},{5,1},{0,2},{1,3},{8,4},{9,5},{2,6},{3,7},{12,8},{13,9},{6,1... | collective-permute-start | bytes 786440 | tf_op jit(solution)/shard_map/ppermute | solution.py:236
  9.0 11.2 %collective-permute-start.15 = (bf16[64,2048]{1,0:T(8,128)(2,1)S(1)}, bf16[64,2048]{1,0:T(8,128)(2,1)S(1)}, u32[]{:S(2)}, u32[]{:S(2)}) collective-permute-start(bf16[64,2048]{1,0:T(8,128)(2,1)S(1)} %collective-permute-done.7.refs_9_), channel_id=1, source_target_pairs={{4,0},{5,1},{0,2},{1,3},{8,4},{9,5},{2,6},{3,7},{12,8},{13,9},{6,1... | collective-permute-start | bytes 786440 | tf_op jit(solution)/shard_map/ppermute | solution.py:234
  10.3 11.2 %collective-permute-start.10 = (bf16[64,2048]{1,0:T(8,128)(2,1)S(1)}, bf16[64,2048]{1,0:T(8,128)(2,1)S(1)}, u32[]{:S(2)}, u32[]{:S(2)}) collective-permute-start(bf16[64,2048]{1,0:T(8,128)(2,1)S(1)} %collective-permute-done.2.refs_4_), channel_id=1, source_target_pairs={{0,4},{1,5},{2,0},{3,1},{4,8},{5,9},{6,2},{7,3},{8,12},{9,13},{10,... | collective-permute-start | bytes 786440 | tf_op jit(solution)/shard_map/ppermute | solution.py:233
  15.6 11.3 %collective-permute-start.11 = (bf16[64,2048]{1,0:T(8,128)(2,1)S(1)}, bf16[64,2048]{1,0:T(8,128)(2,1)S(1)}, u32[]{:S(2)}, u32[]{:S(2)}) collective-permute-start(bf16[64,2048]{1,0:T(8,128)(2,1)S(1)} %collective-permute-done.3.refs_5_), channel_id=1, source_target_pairs={{0,4},{1,5},{2,0},{3,1},{4,8},{5,9},{6,2},{7,3},{8,12},{9,13},{10,... | collective-permute-start | bytes 786440 | tf_op jit(solution)/shard_map/ppermute | solution.py:235
  15.8 11.3 %collective-permute-start.14 = (bf16[64,2048]{1,0:T(8,128)(2,1)S(1)}, bf16[64,2048]{1,0:T(8,128)(2,1)}, u32[]{:S(2)}, u32[]{:S(2)}) collective-permute-start(bf16[64,2048]{1,0:T(8,128)(2,1)S(1)} %collective-permute-done.6.refs_8_), channel_id=1, source_target_pairs={{4,0},{5,1},{0,2},{1,3},{8,4},{9,5},{2,6},{3,7},{12,8},{13,9},{6,1... | collective-permute-start | bytes 786440 | tf_op jit(solution)/shard_map/ppermute | solution.py:236
  20.3 11.3 %collective-permute-start.23 = (bf16[64,2048]{1,0:T(8,128)(2,1)S(1)}, bf16[64,2048]{1,0:T(8,128)(2,1)}, u32[]{:S(2)}, u32[]{:S(2)}) collective-permute-start(bf16[64,2048]{1,0:T(8,128)(2,1)S(1)} %collective-permute-done.15.refs_17_), channel_id=1, source_target_pairs={{4,0},{5,1},{0,2},{1,3},{8,4},{9,5},{2,6},{3,7},{12,8},{13,9},{6,1... | collective-permute-start | bytes 786440 | tf_op jit(solution)/shard_map/ppermute | solution.py:234
  21.6 11.3 %collective-permute-start.18 = (bf16[64,2048]{1,0:T(8,128)(2,1)S(1)}, bf16[64,2048]{1,0:T(8,128)(2,1)}, u32[]{:S(2)}, u32[]{:S(2)}) collective-permute-start(bf16[64,2048]{1,0:T(8,128)(2,1)S(1)} %collective-permute-done.10.refs_12_), channel_id=1, source_target_pairs={{0,4},{1,5},{2,0},{3,1},{4,8},{5,9},{6,2},{7,3},{8,12},{9,13},{10,... | collective-permute-start | bytes 786440 | tf_op jit(solution)/shard_map/ppermute | solution.py:233
  27.0 11.2 %collective-permute-start.19 = (bf16[64,2048]{1,0:T(8,128)(2,1)S(1)}, bf16[64,2048]{1,0:T(8,128)(2,1)}, u32[]{:S(2)}, u32[]{:S(2)}) collective-permute-start(bf16[64,2048]{1,0:T(8,128)(2,1)S(1)} %collective-permute-done.11.refs_13_), channel_id=1, source_target_pairs={{0,4},{1,5},{2,0},{3,1},{4,8},{5,9},{6,2},{7,3},{8,12},{9,13},{10,... | collective-permute-start | bytes 786440 | tf_op jit(solution)/shard_map/ppermute | solution.py:235
  27.1 11.1 %collective-permute-start.22 = (bf16[64,2048]{1,0:T(8,128)(2,1)}, bf16[64,2048]{1,0:T(8,128)(2,1)}, u32[]{:S(2)}, u32[]{:S(2)}) collective-permute-start(bf16[64,2048]{1,0:T(8,128)(2,1)} %collective-permute-done.14.refs_16_), channel_id=1, source_target_pairs={{4,0},{5,1},{0,2},{1,3},{8,4},{9,5},{2,6},{3,7},{12,8},{13,9},{6,1... | collective-permute-start | bytes 786440 | tf_op jit(solution)/shard_map/ppermute | solution.py:236
  31.5 11.0 %collective-permute-start.27 = (bf16[64,2048]{1,0:T(8,128)(2,1)}, bf16[64,2048]{1,0:T(8,128)(2,1)}, u32[]{:S(2)}, u32[]{:S(2)}) collective-permute-start(bf16[64,2048]{1,0:T(8,128)(2,1)} %collective-permute-done.23.refs_25_), channel_id=1, source_target_pairs={{4,0},{5,1},{0,2},{1,3},{8,4},{9,5},{2,6},{3,7},{12,8},{13,9},{6,1... | collective-permute-start | bytes 786440 | tf_op jit(solution)/shard_map/ppermute | solution.py:244
  32.8 11.0 %collective-permute-start.26 = (bf16[64,2048]{1,0:T(8,128)(2,1)}, bf16[64,2048]{1,0:T(8,128)(2,1)}, u32[]{:S(2)}, u32[]{:S(2)}) collective-permute-start(bf16[64,2048]{1,0:T(8,128)(2,1)} %collective-permute-done.18.refs_20_), channel_id=1, source_target_pairs={{0,4},{1,5},{2,0},{3,1},{4,8},{5,9},{6,2},{7,3},{8,12},{9,13},{10,... | collective-permute-start | bytes 786440 | tf_op jit(solution)/shard_map/ppermute | solution.py:243
  43.8 54.6 %all-to-all-start = ((bf16[16,128,384]{2,1,0:T(8,128)(2,1)}), bf16[16,128,384]{2,1,0:T(8,128)(2,1)}, u32[]{:S(2)}, u32[]{:S(2)}) async-start(bf16[16,128,384]{2,1,0:T(8,128)(2,1)} %dispatch.1), calls=%async_computation | async-start | bytes 3145728 | tf_op jit(solution)/shard_map/all_to_all | solution.py:306
  68.7 11.1 %collective-permute-start.32 = (bf16[128,384]{1,0:T(8,128)(2,1)}, bf16[128,384]{1,0:T(8,128)(2,1)S(1)}, u32[]{:S(2)}, u32[]{:S(2)}) collective-permute-start(bf16[128,384]{1,0:T(8,128)(2,1)} %get-tuple-element.37), channel_id=1, source_target_pairs={{0,3},{1,2},{2,1},{3,0},{4,7},{5,6},{6,5},{7,4},{8,11},{9,10},{10,... | collective-permute-start | bytes 294920 | tf_op jit(solution)/shard_map/ppermute | solution.py:267
  70.7 11.7 %collective-permute-start.34 = (bf16[128,384]{1,0:T(8,128)(2,1)}, bf16[128,384]{1,0:T(8,128)(2,1)S(1)}, u32[]{:S(2)}, u32[]{:S(2)}) collective-permute-start(bf16[128,384]{1,0:T(8,128)(2,1)} %get-tuple-element.39), channel_id=1, source_target_pairs={{0,5},{1,4},{2,7},{3,6},{4,1},{5,0},{6,3},{7,2},{8,13},{9,12},{10,... | collective-permute-start | bytes 294920 | tf_op jit(solution)/shard_map/ppermute | solution.py:267
  71.9 16.5 %collective-permute-start.35 = (bf16[128,384]{1,0:T(8,128)(2,1)}, bf16[128,384]{1,0:T(8,128)(2,1)S(1)}, u32[]{:S(2)}, u32[]{:S(2)}) collective-permute-start(bf16[128,384]{1,0:T(8,128)(2,1)} %get-tuple-element.40), channel_id=1, source_target_pairs={{0,6},{1,7},{2,4},{3,5},{4,2},{5,3},{6,0},{7,1},{8,14},{9,15},{10,... | collective-permute-start | bytes 294920 | tf_op jit(solution)/shard_map/ppermute | solution.py:267
  72.7 17.0 %collective-permute-start.36 = (bf16[128,384]{1,0:T(8,128)(2,1)}, bf16[128,384]{1,0:T(8,128)(2,1)S(1)}, u32[]{:S(2)}, u32[]{:S(2)}) collective-permute-start(bf16[128,384]{1,0:T(8,128)(2,1)} %get-tuple-element.41), channel_id=1, source_target_pairs={{0,7},{1,6},{2,5},{3,4},{4,3},{5,2},{6,1},{7,0},{8,15},{9,14},{10,... | collective-permute-start | bytes 294920 | tf_op jit(solution)/shard_map/ppermute | solution.py:267
  79.7 29.1 %collective-permute-start.37 = (bf16[128,384]{1,0:T(8,128)(2,1)}, bf16[128,384]{1,0:T(8,128)(2,1)S(1)}, u32[]{:S(2)}, u32[]{:S(2)}) collective-permute-start(bf16[128,384]{1,0:T(8,128)(2,1)} %get-tuple-element.49), channel_id=1, source_target_pairs={{0,8},{1,9},{2,10},{3,11},{4,12},{5,13},{6,14},{7,15},{8,0},{9,1},... | collective-permute-start | bytes 294920 | tf_op jit(solution)/shard_map/ppermute | solution.py:267
  79.8 29.2 %collective-permute-start.38 = (bf16[128,384]{1,0:T(8,128)(2,1)}, bf16[128,384]{1,0:T(8,128)(2,1)S(1)}, u32[]{:S(2)}, u32[]{:S(2)}) collective-permute-start(bf16[128,384]{1,0:T(8,128)(2,1)} %get-tuple-element.50), channel_id=1, source_target_pairs={{0,9},{1,8},{2,11},{3,10},{4,13},{5,12},{6,15},{7,14},{8,1},{9,0},... | collective-permute-start | bytes 294920 | tf_op jit(solution)/shard_map/ppermute | solution.py:267
  82.4 26.6 %collective-permute-start.39 = (bf16[128,384]{1,0:T(8,128)(2,1)}, bf16[128,384]{1,0:T(8,128)(2,1)S(1)}, u32[]{:S(2)}, u32[]{:S(2)}) collective-permute-start(bf16[128,384]{1,0:T(8,128)(2,1)} %get-tuple-element.51), channel_id=1, source_target_pairs={{0,10},{1,11},{2,8},{3,9},{4,14},{5,15},{6,12},{7,13},{8,2},{9,3},... | collective-permute-start | bytes 294920 | tf_op jit(solution)/shard_map/ppermute | solution.py:267
  88.5 20.9 %collective-permute-start.40 = (bf16[128,384]{1,0:T(8,128)(2,1)}, bf16[128,384]{1,0:T(8,128)(2,1)S(1)}, u32[]{:S(2)}, u32[]{:S(2)}) collective-permute-start(bf16[128,384]{1,0:T(8,128)(2,1)} %get-tuple-element.52), channel_id=1, source_target_pairs={{0,11},{1,10},{2,9},{3,8},{4,15},{5,14},{6,13},{7,12},{8,3},{9,2},... | collective-permute-start | bytes 294920 | tf_op jit(solution)/shard_map/ppermute | solution.py:267
  89.8 19.6 %collective-permute-start.41 = (bf16[128,384]{1,0:T(8,128)(2,1)}, bf16[128,384]{1,0:T(8,128)(2,1)S(1)}, u32[]{:S(2)}, u32[]{:S(2)}) collective-permute-start(bf16[128,384]{1,0:T(8,128)(2,1)} %get-tuple-element.53), channel_id=1, source_target_pairs={{0,12},{1,13},{2,14},{3,15},{4,8},{5,9},{6,10},{7,11},{8,4},{9,5},... | collective-permute-start | bytes 294920 | tf_op jit(solution)/shard_map/ppermute | solution.py:267
  108.9 9.8 %collective-permute-start.43 = (bf16[128,384]{1,0:T(8,128)(2,1)S(1)}, bf16[128,384]{1,0:T(8,128)(2,1)S(1)}, u32[]{:S(2)}, u32[]{:S(2)}) collective-permute-start(bf16[128,384]{1,0:T(8,128)(2,1)S(1)} %copy-done.27), channel_id=1, source_target_pairs={{0,14},{1,15},{2,12},{3,13},{4,10},{5,11},{6,8},{7,9},{8,6},{9,7},... | collective-permute-start | bytes 294920 | tf_op jit(solution)/shard_map/ppermute | solution.py:267
  109.0 12.0 %collective-permute-start.44 = (bf16[128,384]{1,0:T(8,128)(2,1)S(1)}, bf16[128,384]{1,0:T(8,128)(2,1)S(1)}, u32[]{:S(2)}, u32[]{:S(2)}) collective-permute-start(bf16[128,384]{1,0:T(8,128)(2,1)S(1)} %copy-done.26), channel_id=1, source_target_pairs={{0,15},{1,14},{2,13},{3,12},{4,11},{5,10},{6,9},{7,8},{8,7},{9,6},... | collective-permute-start | bytes 294920 | tf_op jit(solution)/shard_map/ppermute | solution.py:267
  (51 other events, 553.8 us)
